TPU v7x, 32 devices: a whole 2x2x4 slice. The times are simulated.
32 devices in a mesh: leaf: 8 (over z, y), cols: 4 (over x, core).
Axes of the slice: x: 2, y: 2, z: 4, core: 2. Of those that a mesh axis runs over, the one named last changes fastest.
Arguments:
- points: bfloat16 [32768, 64], P('leaf', 'cols'), may hold values from -6 to 6
- weights: bfloat16 [32768, 1024], P('leaf', 'cols'), may hold values from -6 to 6
- leaf_basis: bfloat16 [8192, 1024], P('leaf'), may hold values from -0.1875 to 0.1875
- dev_transfer: bfloat16 [2048, 1024], P('leaf'), may hold values from -0.1875 to 0.1875
- group_transfer: bfloat16 [512, 1024], P('leaf'), may hold values from -0.1875 to 0.1875
- leaf_skeleton: int32 [32, 256], P('leaf'), may hold values from 0 to 1023, as said below
- dev_skeleton: int32 [8, 256], P('leaf'), may hold values from 0 to 1023, as said below
- group_skeleton: int32 [2, 256], replicated, may hold values from 0 to 1023, as said below
- near_list: int32 [32, 3], P('leaf'), may hold values from 0 to 31, as said below
- near_count: int32 [32], P('leaf'), may hold values from 1 to 3
Outputs:
- potentials: float32 [32768, 1024], P('leaf', 'cols')
Inputs may be any that keep to these rules, and one draw needn't show every extreme that they name: `leaf_skeleton`: each row holds 256 distinct point numbers within the leaf. `dev_skeleton`: each row holds 256 distinct numbers into the 1024 skeleton points of the node's children, in child order. `group_skeleton`: each row holds 256 distinct numbers into the 1024 skeleton points of the node's children, in child order. `near_list`: row l names leaves of the first-level node holding leaf l and of the first-level nodes just before and after it; its first entry is l itself and its first near_count[l] entries are distinct; later entries are leaf numbers that are not used.
All inputs are finite; a program needn't handle non-finite values.
Results may differ from a plain program's by a relative error of at most 0.005.
Values may be sent and summed in bfloat16 or wider, within the bound.
A program may use at most 128 MiB of HBM per device.

v0:
```python
import jax
import jax.numpy as jnp
from jax import lax
from jax.sharding import PartitionSpec as P

LEAF = 1024
NEARMAX = 3


SHARPNESS = 2.0


def swapped(value, axis, stride):
    mask = 2**stride
    pairs = [(source, source ^ mask) for source in range(lax.axis_size(axis))]
    return lax.ppermute(value, axis, pairs)


def with_halo(array, sides, width):
    for axis, dim in sides:
        count, length = (lax.axis_size(axis), array.shape[dim])
        up = [(i, (i + 1) % count) for i in range(count - 1)]
        down = [(j, i) for i, j in up]
        last = lax.slice_in_dim(array, length - width, length, axis=dim)
        initial = lax.slice_in_dim(array, 0, width, axis=dim)
        before = lax.ppermute(last, axis, up)
        after = lax.ppermute(initial, axis, down)
        array = jnp.concatenate([before, array, after], axis=dim)
    return array


def kernel_matrix(row_points, col_points):
    inner_prod = jnp.einsum("ad,bd->ab", row_points, col_points, preferred_element_type=jnp.float32)
    row_float = row_points.astype(jnp.float32)
    col_float = col_points.astype(jnp.float32)
    row_norms = jnp.sum(row_float * row_float, axis=1)
    col_norms = jnp.sum(col_float * col_float, axis=1)
    return jnp.exp(
        -SHARPNESS
        / row_points.shape[1]
        * (row_norms[:, None] + col_norms[None, :] - 2.0 * inner_prod)
    )


def per_device(
    points,
    weights,
    leaf_basis,
    dev_transfer,
    group_transfer,
    leaf_skeleton,
    dev_skeleton,
    group_skeleton,
    near_list,
    near_count,
):
    position = lax.axis_index("leaf")
    member = position % 4
    group_no = position // 4
    quarter = group_transfer.shape[0]
    skel_rank = leaf_skeleton.shape[1]
    held = group_transfer.reshape(quarter, 4, skel_rank).transpose(1, 0, 2)[:, None]
    for flip_bit in (1, 0):
        dest_count = held.shape[0]
        halves = held.reshape(2, dest_count // 2, held.shape[1], quarter, skel_rank)
        upper_half = position // (1 << flip_bit) % 2 == 1
        kept_part = jnp.where(upper_half, halves[1], halves[0])
        sent_part = jnp.where(upper_half, halves[0], halves[1])
        arrived = swapped(sent_part, "leaf", flip_bit)
        paired = jnp.where(
            upper_half,
            jnp.stack([arrived, kept_part], axis=2),
            jnp.stack([kept_part, arrived], axis=2),
        )
        held = paired.reshape(dest_count // 2, paired.shape[1] * 2, quarter, skel_rank)
    own_transfer = held.reshape(4 * quarter, skel_rank)
    coordinates = lax.all_gather(points, "cols", axis=1, tiled=True)
    dev_rows, feat_width = coordinates.shape
    col_width = weights.shape[1]
    leaf_count = dev_rows // LEAF
    leaf_points = coordinates.reshape(leaf_count, LEAF, feat_width)
    leaf_weights = weights.reshape(leaf_count, LEAF, col_width)
    leaf_maps = leaf_basis.reshape(leaf_count, skel_rank, LEAF)
    leaf_skel = (
        jnp.einsum("lrp,lpc->lrc", leaf_maps, leaf_weights, preferred_element_type=jnp.float32)
        .astype(jnp.bfloat16)
        .reshape(leaf_count * skel_rank, col_width)
    )
    leaf_coords = jnp.take_along_axis(leaf_points, leaf_skeleton[:, :, None], axis=1).reshape(
        leaf_count * skel_rank, feat_width
    )
    row_block = jnp.arange(leaf_count * skel_rank, dtype=jnp.int32) // skel_rank
    leaf_coupling = jnp.where(
        row_block[:, None] != row_block[None, :], kernel_matrix(leaf_coords, leaf_coords), 0.0
    ).astype(jnp.bfloat16)
    leaf_field = jnp.dot(leaf_coupling, leaf_skel, preferred_element_type=jnp.float32)
    node_skel = jnp.dot(dev_transfer, leaf_skel, preferred_element_type=jnp.float32).astype(
        jnp.bfloat16
    )
    node_coords = jnp.take(leaf_coords, dev_skeleton[0], axis=0)
    packed = jnp.concatenate([node_skel, node_coords], axis=1)
    family = packed
    for flip_bit in (0, 1):
        partner = swapped(family, "leaf", flip_bit)
        upper_half = position // (1 << flip_bit) % 2 == 1
        family = jnp.where(
            upper_half,
            jnp.concatenate([partner, family], axis=0),
            jnp.concatenate([family, partner], axis=0),
        )
    family_skel = family[:, :col_width]
    family_coords = family[:, col_width:]
    col_block = jnp.arange(4 * skel_rank, dtype=jnp.int32) // skel_rank
    node_coupling = jnp.where(
        col_block[None, :] != member, kernel_matrix(node_coords, family_coords), 0.0
    ).astype(jnp.bfloat16)
    node_field = jnp.dot(node_coupling, family_skel, preferred_element_type=jnp.float32)
    chosen = lax.dynamic_index_in_dim(group_skeleton, group_no, 0, keepdims=False)
    group_coords = jnp.take(family_coords, chosen, axis=0)
    quarter_skel = jnp.dot(group_transfer, family_skel, preferred_element_type=jnp.float32).astype(
        jnp.bfloat16
    )
    quarter_coords = lax.dynamic_slice_in_dim(group_coords, member * quarter, quarter, 0)
    all_groups = lax.all_gather(
        jnp.concatenate([quarter_skel, quarter_coords], axis=1), "leaf", axis=0, tiled=True
    )
    top_block = jnp.arange(all_groups.shape[0], dtype=jnp.int32) // skel_rank
    top_coupling = jnp.where(
        top_block[None, :] != group_no, kernel_matrix(group_coords, all_groups[:, col_width:]), 0.0
    ).astype(jnp.bfloat16)
    top_field = jnp.dot(
        top_coupling, all_groups[:, :col_width], preferred_element_type=jnp.float32
    ).astype(jnp.bfloat16)
    shares = jnp.einsum("rk,rc->kc", own_transfer, top_field, preferred_element_type=jnp.float32)
    node_total = (node_field + shares).astype(jnp.bfloat16)
    leaf_total = (
        leaf_field
        + jnp.einsum("rk,rc->kc", dev_transfer, node_total, preferred_element_type=jnp.float32)
    ).astype(jnp.bfloat16)
    far_part = jnp.einsum(
        "lrp,lrc->lpc",
        leaf_maps,
        leaf_total.reshape(leaf_count, skel_rank, col_width),
        preferred_element_type=jnp.float32,
    )
    halo_cargo = jnp.concatenate([coordinates, weights], axis=1)
    extended = with_halo(halo_cargo, (("leaf", 0),), dev_rows)
    first_leaf = (position - 1) * leaf_count
    near_blocks = []
    for leaf_no in range(leaf_count):
        near_sum = jnp.zeros((LEAF, col_width), jnp.float32)
        for slot_no in range(NEARMAX):
            source = near_list[leaf_no, slot_no] - first_leaf
            rows_block = lax.dynamic_slice_in_dim(extended, source * LEAF, LEAF, 0)
            kernel_block = kernel_matrix(leaf_points[leaf_no], rows_block[:, :feat_width]).astype(
                jnp.bfloat16
            )
            active_slot = (slot_no < near_count[leaf_no]).astype(jnp.float32)
            near_sum = near_sum + active_slot * jnp.dot(
                kernel_block, rows_block[:, feat_width:], preferred_element_type=jnp.float32
            )
        near_blocks.append(near_sum)
    near_part = jnp.stack(near_blocks)
    return (near_part + far_part).reshape(dev_rows, col_width)


def solution(mesh):
    in_specs = (
        P("leaf", "cols"),
        P("leaf", "cols"),
        P("leaf", None),
        P("leaf", None),
        P("leaf", None),
        P("leaf", None),
        P("leaf", None),
        P(),
        P("leaf", None),
        P("leaf"),
    )
    out_specs = P("leaf", "cols")
    return jax.shard_map(
        per_device, mesh=mesh, in_specs=in_specs, out_specs=out_specs, check_vma=False
    )
```

profile of v0, /device:TPU:0, one launch (start us, length us, event | category | flops | bytes accessed | tf_op | source)
XLA Modules:
  0.0 270.7 jit_solution(11807811734899606962)
XLA Ops:
  0.0 8.9 %all_gather.6 = bf16[4096,64]{0,1:T(8,128)(2,1)S(1)} all-gather(bf16[4096,16]{0,1:T(8,128)(2,1)} %param.12), channel_id=1, replica_groups=mesh['leaf'=8,'cols'=4] {'cols'}, dimensions={1}, use_global_device_ids=true | all-gather | bytes 655360 | tf_op jit(solution)/shard_map/all_gather | solution.py:77
  9.0 4.1 %copy.120 = bf16[4096,256]{0,1:T(8,128)(2,1)} copy(bf16[4096,256]{1,0:T(8,128)(2,1)} %param.13) | data formatting | bytes 4194304 | tf_op args[1]
  13.1 3.4 %pad_maximum_fusion.1 = bf16[4096,320]{0,1:T(8,128)(2,1)} fusion(bf16[4096,256]{0,1:T(8,128)(2,1)} %copy.120, bf16[4096,64]{0,1:T(8,128)(2,1)S(1)} %all_gather.6), kind=kLoop, calls=%fused_computation.54 | loop fusion | flops 5242880 | bytes 5242880 | tf_op jit(solution)/shard_map/concatenate | solution.py:146
  16.5 5.0 %collective-permute-start = (bf16[4096,320]{0,1:T(8,128)(2,1)}, bf16[4096,320]{0,1:T(8,128)(2,1)}, u32[]{:S(2)}, u32[]{:S(2)}) collective-permute-start(bf16[4096,320]{0,1:T(8,128)(2,1)} %pad_maximum_fusion.1), channel_id=1, source_target_pairs={{0,4},{4,8},{8,12},{12,16},{16,20},{20,24},{24,28},{1,5},{5,9},{9,... | collective-permute-start | bytes 7864328 | tf_op jit(solution)/shard_map/ppermute | solution.py:26
  21.5 1.3 collective-permute-start.1
  22.8 1.3 copy.145
  24.8 12.4 %gather_fusion = bf16[1024,64]{1,0:T(8,128)(2,1)S(1)} fusion(bf16[4,1024,64]{2,1,0:T(8,128)(2,1)} %bitcast.265, s32[1024]{0:T(1024)S(1)} %bitcast.264), kind=kCustom, calls=%fused_computation.2 | custom fusion | bytes 270336 | tf_op jit(solution)/shard_map/jit(take_along_axis)/gather | solution.py:89
  37.4 0.9 gather_fusion.1
  38.9 2.3 convolution_convert_fusion
  42.8 2.7 collective-permute-start.2
  45.5 0.8 fusion.171
  46.4 0.7 multiply_reduce_fusion.18
  47.5 0.7 fusion.240
  48.9 4.2 %fusion.64 = f32[1024,256]{1,0:T(8,128)} fusion(bf16[1024,256]{1,0:T(8,128)(2,1)} %bitcast.270, bf16[1024,64]{1,0:T(8,128)(2,1)S(1)} %bitcast.273, f32[1024]{0:T(1024)S(1)} %bitcast.283, s32[1024]{0:T(1024)S(1)} %add_select_fusion), kind=kOutput, calls=%fused_computation.86 | convolution fusion | flops 678428672 | bytes 1712128 | tf_op jit(solution)/shard_map/dot_general | solution.py:96
  69.2 14.1 %collective-permute-done.4 = bf16[2,1,64,256]{3,0,2,1:T(2,128)(2,1)S(1)} collective-permute-done((bf16[2,1,64,256]{3,0,2,1:T(2,128)(2,1)}, bf16[2,1,64,256]{3,0,2,1:T(2,128)(2,1)S(1)}, u32[]{:S(2)}, u32[]{:S(2)}) %collective-permute-start.4) | collective-permute-done | bytes 65568 | tf_op jit(solution)/shard_map/ppermute | solution.py:16
  83.5 53.1 %collective-permute-done.2 = bf16[256,320]{0,1:T(8,128)(2,1)} collective-permute-done((bf16[256,320]{0,1:T(8,128)(2,1)}, bf16[256,320]{0,1:T(8,128)(2,1)}, u32[]{:S(2)}, u32[]{:S(2)}) %collective-permute-start.2) | collective-permute-done | bytes 163872 | tf_op jit(solution)/shard_map/ppermute | solution.py:16
  136.6 1.1 maximum_select_fusion.1
  137.6 3.5 %collective-permute-start.3 = (bf16[512,320]{0,1:T(8,128)(2,1)S(1)}, bf16[512,320]{0,1:T(8,128)(2,1)S(1)}, u32[]{:S(2)}, u32[]{:S(2)}) collective-permute-start(bf16[512,320]{0,1:T(8,128)(2,1)S(1)} %maximum_select_fusion.1), channel_id=1, source_target_pairs={{0,8},{4,12},{8,0},{12,4},{16,24},{20,28},{24,16},{28,20},{1,9},{5... | collective-permute-start | bytes 983048 | tf_op jit(solution)/shard_map/ppermute | solution.py:16
  142.7 3.1 %collective-permute-done.5 = bf16[1,2,64,256]{3,2,1,0:T(8,128)(2,1)S(1)} collective-permute-done((bf16[1,2,64,256]{3,2,1,0:T(8,128)(2,1)S(1)}, bf16[1,2,64,256]{3,2,1,0:T(8,128)(2,1)S(1)}, u32[]{:S(2)}, u32[]{:S(2)}) %collective-permute-start.5) | collective-permute-done | bytes 65568 | tf_op jit(solution)/shard_map/ppermute | solution.py:16
  146.5 2.6 collective-permute-done.3
  149.2 0.9 copy-done.4
  150.4 0.9 gather_fusion.2
  151.2 0.8 multiply_reduce_fusion.19
  152.1 1.3 fusion.91
  153.4 0.9 multiply_reduce_fusion.2
  154.4 31.8 %all_gather.7 = bf16[512,320]{1,0:T(8,128)(2,1)S(1)} all-gather(bf16[64,320]{1,0:T(8,128)(2,1)S(1)} %pad_maximum_fusion.3), channel_id=1, replica_groups=mesh['leaf'=8,'cols'=4] {'leaf'}, dimensions={0}, use_global_device_ids=true | all-gather | bytes 368640 | tf_op jit(solution)/shard_map/all_gather | solution.py:124
  186.1 0.8 copy-done.5
  187.1 2.1 fusion.88
  189.2 1.2 fusion.242
  190.4 2.4 fusion.89
  192.8 2.5 fusion.79
  195.3 10.8 %pad_maximum_fusion = bf16[12288,320]{0,1:T(8,128)(2,1)S(1)} fusion(bf16[4096,320]{0,1:T(8,128)(2,1)} %collective-permute-done.1, bf16[4096,256]{0,1:T(8,128)(2,1)} %copy.120, bf16[4096,64]{0,1:T(8,128)(2,1)S(1)} %all_gather.6, bf16[4096,320]{0,1:T(8,128)(2,1)} %collective-permute-done), kind=kLoop, calls=%fused_computation.3 | loop fusion | flops 31457280 | bytes 15728640 | tf_op jit(solution)/shard_map/concatenate | solution.py:28
  206.1 3.1 %copy-done.1 = bf16[12288,320]{0,1:T(8,128)(2,1)} copy-done((bf16[12288,320]{0,1:T(8,128)(2,1)}, bf16[12288,320]{0,1:T(8,128)(2,1)S(1)}, u32[]{:S(2)}) %copy-start.1) | copy-done | bytes 7864344
  209.6 2.4 broadcast_add_fusion
  211.9 5.3 %copy.122 = f32[1024,1024]{0,1:T(8,128)} copy(f32[1024,1024]{1,0:T(8,128)} %broadcast_add_fusion) | data formatting | bytes 8388608 | tf_op jit(solution)/shard_map/add | solution.py:41
  217.3 3.7 %fusion.58 = f32[1024,256]{1,0:T(8,128)} fusion(f32[1024]{0:T(1024)S(1)} %get-tuple-element.17, f32[1024]{0:T(1024)S(1)} %get-tuple-element.18, bf16[12288,320]{0,1:T(8,128)(2,1)} %copy-done.1, s32[]{:T(128)S(6)} %select_n.248, s32[]{:T(128)S(6)} %add.379, f32[]{:T(128)} %bitcast.3, bf16[4096,64]{0,1:T(8,128)(2,1)S(1)} %all_gather.6), kind=kOutput, calls=%fused_computation.78 | convolution fusion | flops 676593664 | bytes 1845248 | tf_op jit(solution)/shard_map/dot_general | solution.py:159
  220.9 3.6 %fusion.57 = f32[1024,256]{1,0:T(8,128)} fusion(f32[1024]{0:T(1024)S(1)} %get-tuple-element.16, f32[1024]{0:T(1024)S(1)} %get-tuple-element.18, bf16[12288,320]{0,1:T(8,128)(2,1)} %copy-done.1, s32[]{:T(128)S(6)} %select_n.249, s32[]{:T(128)S(6)} %add.379, f32[]{:T(128)} %bitcast.6, bf16[4096,64]{0,1:T(8,128)(2,1)S(1)} %all_gather.6), kind=kOutput, calls=%fused_computation.77 | convolution fusion | flops 676593664 | bytes 1845248 | tf_op jit(solution)/shard_map/dot_general | solution.py:159
  224.6 3.7 %fusion.55 = f32[1024,256]{1,0:T(8,128)} fusion(f32[1024]{0:T(1024)S(1)} %get-tuple-element.14, f32[1024]{0:T(1024)S(1)} %copy-done.14, bf16[12288,320]{0,1:T(8,128)(2,1)} %copy-done.1, s32[]{:T(128)S(6)} %select_n.251, s32[]{:T(128)S(6)} %add.379, f32[]{:T(128)} %bitcast.13, bf16[4096,64]{0,1:T(8,128)(2,1)S(1)} %all_gather.6), kind=kOutput, calls=%fused_computation.75 | convolution fusion | flops 676593664 | bytes 1845248 | tf_op jit(solution)/shard_map/dot_general | solution.py:159
  228.2 3.7 %fusion.54 = f32[1024,256]{1,0:T(8,128)} fusion(f32[1024]{0:T(1024)S(1)} %get-tuple-element.13, f32[1024]{0:T(1024)S(1)} %copy-done.14, bf16[12288,320]{0,1:T(8,128)(2,1)} %copy-done.1, s32[]{:T(128)S(6)} %select_n.252, s32[]{:T(128)S(6)} %add.379, f32[]{:T(128)} %bitcast.16, bf16[4096,64]{0,1:T(8,128)(2,1)S(1)} %all_gather.6), kind=kOutput, calls=%fused_computation.74 | convolution fusion | flops 676593664 | bytes 1845248 | tf_op jit(solution)/shard_map/dot_general | solution.py:159
  231.9 3.7 %fusion.52 = f32[1024,256]{1,0:T(8,128)} fusion(f32[1024]{0:T(1024)S(1)} %get-tuple-element.11, f32[1024]{0:T(1024)S(1)} %get-tuple-element.20, bf16[12288,320]{0,1:T(8,128)(2,1)} %copy-done.1, s32[]{:T(128)S(6)} %select_n.254, s32[]{:T(128)S(6)} %add.379, f32[]{:T(128)} %bitcast.23, bf16[4096,64]{0,1:T(8,128)(2,1)S(1)} %all_gather.6), kind=kOutput, calls=%fused_computation.72 | convolution fusion | flops 676593664 | bytes 1845248 | tf_op jit(solution)/shard_map/dot_general | solution.py:159
  235.6 3.7 %fusion.51 = f32[1024,256]{1,0:T(8,128)} fusion(f32[1024]{0:T(1024)S(1)} %get-tuple-element.10, f32[1024]{0:T(1024)S(1)} %get-tuple-element.20, bf16[12288,320]{0,1:T(8,128)(2,1)} %copy-done.1, s32[]{:T(128)S(6)} %select_n.255, s32[]{:T(128)S(6)} %add.379, f32[]{:T(128)} %bitcast.26, bf16[4096,64]{0,1:T(8,128)(2,1)S(1)} %all_gather.6), kind=kOutput, calls=%fused_computation.71 | convolution fusion | flops 676593664 | bytes 1845248 | tf_op jit(solution)/shard_map/dot_general | solution.py:159
  239.3 3.7 %fusion.49 = f32[1024,256]{1,0:T(8,128)} fusion(f32[1024]{0:T(1024)S(1)} %get-tuple-element.8, f32[1024]{0:T(1024)S(1)} %get-tuple-element.19, bf16[12288,320]{0,1:T(8,128)(2,1)} %copy-done.1, s32[]{:T(128)S(6)} %select_n.257, s32[]{:T(128)S(6)} %add.379, f32[]{:T(128)} %bitcast.33, bf16[4096,64]{0,1:T(8,128)(2,1)S(1)} %all_gather.6), kind=kOutput, calls=%fused_computation.69 | convolution fusion | flops 676593664 | bytes 1845248 | tf_op jit(solution)/shard_map/dot_general | solution.py:159
  243.0 3.9 %fusion.48 = f32[1024,256]{1,0:T(8,128)} fusion(f32[1024]{0:T(1024)S(1)} %get-tuple-element.7, f32[1024]{0:T(1024)S(1)} %get-tuple-element.19, bf16[12288,320]{0,1:T(8,128)(2,1)} %copy-done.1, s32[]{:T(128)S(6)} %select_n.258, s32[]{:T(128)S(6)} %add.379, f32[]{:T(128)} %bitcast.36, bf16[4096,64]{0,1:T(8,128)(2,1)S(1)} %all_gather.6), kind=kOutput, calls=%fused_computation.68 | convolution fusion | flops 676593664 | bytes 1845248 | tf_op jit(solution)/shard_map/dot_general | solution.py:159
  246.9 5.7 %fusion.68 = f32[1,1024,256]{2,1,0:T(8,128)} fusion(f32[1024,256]{1,0:T(8,128)} %fusion.57, f32[1024,256]{1,0:T(8,128)} %fusion.58, f32[1024,1024]{0,1:T(8,128)} %copy.122, bf16[12288,320]{0,1:T(8,128)(2,1)} %copy-done.1, s32[]{:T(128)S(6)} %select_n.247, s32[]{:T(128)S(6)} %add.379, f32[]{:T(128)} %bitcast, bf16[4096,64]{0,1:T(8,128)(2,1)S(1)} %all_gather.6), kind=kOutput, calls=%fused_computation.90 | convolution fusion | flops 676069376 | bytes 8128512 | tf_op jit(solution)/shard_map/dot_general | solution.py:159
  252.6 4.3 %fusion.71 = f32[1,1024,256]{2,1,0:T(8,128)} fusion(f32[1024,256]{1,0:T(8,128)} %fusion.54, f32[1024,256]{1,0:T(8,128)} %fusion.55, f32[1024]{0:T(1024)S(1)} %get-tuple-element.15, f32[1024]{0:T(1024)S(1)} %copy-done.14, bf16[12288,320]{0,1:T(8,128)(2,1)} %copy-done.1, s32[]{:T(128)S(6)} %select_n.250, s32[]{:T(128)S(6)} %add.379, f32[]{:T(128)} %bitcast.10, ...), kind=kOutput, calls=%fused_computation.93 | convolution fusion | flops 677117952 | bytes 3942400 | tf_op jit(solution)/shard_map/dot_general | solution.py:159
  256.9 4.3 %fusion.74 = f32[1,1024,256]{2,1,0:T(8,128)} fusion(f32[1024,256]{1,0:T(8,128)} %fusion.51, f32[1024,256]{1,0:T(8,128)} %fusion.52, f32[1024]{0:T(1024)S(1)} %get-tuple-element.12, f32[1024]{0:T(1024)S(1)} %get-tuple-element.20, bf16[12288,320]{0,1:T(8,128)(2,1)} %copy-done.1, s32[]{:T(128)S(6)} %select_n.253, s32[]{:T(128)S(6)} %add.379, f32[]{:T(128)} %bitcast.20, ...), kind=kOutput, calls=%fused_computation.96 | convolution fusion | flops 677117952 | bytes 3942400 | tf_op jit(solution)/shard_map/dot_general | solution.py:159
  261.2 4.4 %fusion.77 = f32[1,1024,256]{2,1,0:T(8,128)} fusion(f32[1024,256]{1,0:T(8,128)} %fusion.48, f32[1024,256]{1,0:T(8,128)} %fusion.49, f32[1024]{0:T(1024)S(1)} %get-tuple-element.9, f32[1024]{0:T(1024)S(1)} %get-tuple-element.19, bf16[12288,320]{0,1:T(8,128)(2,1)} %copy-done.1, s32[]{:T(128)S(6)} %select_n.256, s32[]{:T(128)S(6)} %add.379, f32[]{:T(128)} %bitcast.30, ...), kind=kOutput, calls=%fused_computation.99 | convolution fusion | flops 677117952 | bytes 3942400 | tf_op jit(solution)/shard_map/dot_general | solution.py:159
  265.6 5.1 %maximum_add_fusion = f32[4,1024,256]{2,1,0:T(8,128)} fusion(f32[1,1024,256]{2,1,0:T(8,128)} %fusion.77, f32[1,1024,256]{2,1,0:T(8,128)} %fusion.74, f32[1,1024,256]{2,1,0:T(8,128)} %fusion.71, f32[1,1024,256]{2,1,0:T(8,128)} %fusion.68, bf16[4,256,256]{2,1,0:T(8,128)(2,1)S(1)} %bitcast.268, bf16[4,256,1024]{2,1,0:T(8,128)(2,1)S(1)} %bitcast.263), kind=kOutput, calls=%fused_computation.4 | convolution fusion | flops 541065216 | bytes 11010048 | tf_op jit(solution)/shard_map/lrp,lrc->lpc/dot_general | solution.py:140
  (74 shorter events, 8.2 us)
Async XLA Ops:
  0.0 38.9 %copy-start = (bf16[1024,1024]{1,0:T(8,128)(2,1)S(1)}, bf16[1024,1024]{1,0:T(8,128)(2,1)}, u32[]{:S(2)}) copy-start(bf16[1024,1024]{1,0:T(8,128)(2,1)} %param.14) | copy-start | bytes 6291460
  13.1 11.0 %copy-start.12 = (s32[4,256]{1,0:T(4,128)S(1)}, s32[4,256]{1,0:T(4,128)}, u32[]{:S(2)}) copy-start(s32[4,256]{1,0:T(4,128)} %param.17) | copy-start | bytes 12292
  13.1 11.0 %copy-start.15 = (s32[1,256]{1,0:T(1,128)S(1)}, s32[1,256]{1,0:T(1,128)}, u32[]{:S(2)}) copy-start(s32[1,256]{1,0:T(1,128)} %param.18) | copy-start | bytes 3076
  13.1 11.1 %copy-start.17 = (s32[2,256]{1,0:T(2,128)S(1)}, s32[2,256]{1,0:T(2,128)}, u32[]{:S(2)}) copy-start(s32[2,256]{1,0:T(2,128)} %param.19) | copy-start | bytes 6148
  16.5 178.7 %collective-permute-start = (bf16[4096,320]{0,1:T(8,128)(2,1)}, bf16[4096,320]{0,1:T(8,128)(2,1)}, u32[]{:S(2)}, u32[]{:S(2)}) collective-permute-start(bf16[4096,320]{0,1:T(8,128)(2,1)} %pad_maximum_fusion.1), channel_id=1, source_target_pairs={{0,4},{4,8},{8,12},{12,16},{16,20},{20,24},{24,28},{1,5},{5,9},{9,... | collective-permute-start | bytes 7864328 | tf_op jit(solution)/shard_map/ppermute | solution.py:26
  21.5 173.8 %collective-permute-start.1 = (bf16[4096,320]{0,1:T(8,128)(2,1)}, bf16[4096,320]{0,1:T(8,128)(2,1)}, u32[]{:S(2)}, u32[]{:S(2)}) collective-permute-start(bf16[4096,320]{0,1:T(8,128)(2,1)} %pad_maximum_fusion.1), channel_id=1, source_target_pairs={{4,0},{8,4},{12,8},{16,12},{20,16},{24,20},{28,24},{5,1},{9,5},{13... | collective-permute-start | bytes 7864328 | tf_op jit(solution)/shard_map/ppermute | solution.py:27
  37.2 8.3 %copy-start.10 = (bf16[64,1024]{1,0:T(8,128)(2,1)S(1)}, bf16[64,1024]{1,0:T(8,128)(2,1)}, u32[]{:S(2)}) copy-start(bf16[64,1024]{1,0:T(8,128)(2,1)} %param.16) | copy-start | bytes 393220
  38.3 2.9 %copy-start.2 = (bf16[256,1024]{1,0:T(8,128)(2,1)S(1)}, bf16[256,1024]{1,0:T(8,128)(2,1)}, u32[]{:S(2)}) copy-start(bf16[256,1024]{1,0:T(8,128)(2,1)} %param.15) | copy-start | bytes 1572868
  38.3 9.2 %copy-start.11 = (s32[4,3]{1,0:T(4,128)S(1)}, s32[4,3]{1,0:T(4,128)}, u32[]{:S(2)}) copy-start(s32[4,3]{1,0:T(4,128)} %param.20) | copy-start | bytes 148
  38.4 9.9 %copy-start.13 = (s32[4]{0:T(128)S(1)}, s32[4]{0:T(128)}, u32[]{:S(2)}) copy-start(s32[4]{0:T(128)} %param.21) | copy-start | bytes 52
  38.9 97.6 %copy-start.8 = (bf16[256,64]{0,1:T(8,128)(2,1)}, bf16[256,64]{0,1:T(8,128)(2,1)S(1)}, u32[]{:S(2)}) copy-start(bf16[256,64]{0,1:T(8,128)(2,1)S(1)} %get-tuple-element.23) | copy-start | bytes 98308
  41.3 0.8 copy-start.7
  42.8 93.8 %collective-permute-start.2 = (bf16[256,320]{0,1:T(8,128)(2,1)}, bf16[256,320]{0,1:T(8,128)(2,1)}, u32[]{:S(2)}, u32[]{:S(2)}) collective-permute-start(bf16[256,320]{0,1:T(8,128)(2,1)} %pad_maximum_fusion.2), channel_id=1, source_target_pairs={{0,4},{4,0},{8,12},{12,8},{16,20},{20,16},{24,28},{28,24},{1,5},{5... | collective-permute-start | bytes 491528 | tf_op jit(solution)/shard_map/ppermute | solution.py:16
  46.3 37.0 %collective-permute-start.4 = (bf16[2,1,64,256]{3,0,2,1:T(2,128)(2,1)}, bf16[2,1,64,256]{3,0,2,1:T(2,128)(2,1)S(1)}, u32[]{:S(2)}, u32[]{:S(2)}) collective-permute-start(bf16[2,1,64,256]{3,0,2,1:T(2,128)(2,1)} %get-tuple-element.30), channel_id=1, source_target_pairs={{0,8},{4,12},{8,0},{12,4},{16,24},{20,28},{24,16},{28,20},{1,9},{5... | collective-permute-start | bytes 196616 | tf_op jit(solution)/shard_map/ppermute | solution.py:16
  137.6 11.4 %collective-permute-start.3 = (bf16[512,320]{0,1:T(8,128)(2,1)S(1)}, bf16[512,320]{0,1:T(8,128)(2,1)S(1)}, u32[]{:S(2)}, u32[]{:S(2)}) collective-permute-start(bf16[512,320]{0,1:T(8,128)(2,1)S(1)} %maximum_select_fusion.1), channel_id=1, source_target_pairs={{0,8},{4,12},{8,0},{12,4},{16,24},{20,28},{24,16},{28,20},{1,9},{5... | collective-permute-start | bytes 983048 | tf_op jit(solution)/shard_map/ppermute | solution.py:16
  141.5 4.3 %collective-permute-start.5 = (bf16[1,2,64,256]{3,2,1,0:T(8,128)(2,1)S(1)}, bf16[1,2,64,256]{3,2,1,0:T(8,128)(2,1)S(1)}, u32[]{:S(2)}, u32[]{:S(2)}) collective-permute-start(bf16[1,2,64,256]{3,2,1,0:T(8,128)(2,1)S(1)} %bitcast.275), channel_id=1, source_target_pairs={{0,4},{4,0},{8,12},{12,8},{16,20},{20,16},{24,28},{28,24},{1,5},{5... | collective-permute-start | bytes 196616 | tf_op jit(solution)/shard_map/ppermute | solution.py:16
  149.2 0.9 copy-start.4
  150.1 42.6 %copy-start.3 = (bf16[256,1024]{1,0:T(8,128)(2,1)S(1)}, bf16[256,1024]{1,0:T(8,128)(2,1)}, u32[]{:S(2)}) copy-start(bf16[256,1024]{1,0:T(8,128)(2,1)} %param.15) | copy-start | bytes 1572868
  150.3 40.0 %copy-start.9 = (bf16[256,64]{0,1:T(8,128)(2,1)S(1)}, bf16[256,64]{0,1:T(8,128)(2,1)}, u32[]{:S(2)}) copy-start(bf16[256,64]{0,1:T(8,128)(2,1)} %copy-done.8) | copy-start | bytes 98308
  150.3 40.0 %copy-start.16 = (f32[256]{0:T(256)S(1)}, f32[256]{0:T(256)}, u32[]{:S(2)}) copy-start(f32[256]{0:T(256)} %get-tuple-element.22) | copy-start | bytes 3076
  150.3 40.0 %copy-start.18 = (pred[1024]{0:T(1024)(128)(4,1)S(1)}, pred[1024]{0:T(1024)(128)(4,1)}, u32[]{:S(2)}) copy-start(pred[1024]{0:T(1024)(128)(4,1)} %broadcast_compare_fusion) | copy-start | bytes 3076
  186.1 0.8 copy-start.5
  206.1 3.1 %copy-start.1 = (bf16[12288,320]{0,1:T(8,128)(2,1)}, bf16[12288,320]{0,1:T(8,128)(2,1)S(1)}, u32[]{:S(2)}) copy-start(bf16[12288,320]{0,1:T(8,128)(2,1)S(1)} %pad_maximum_fusion) | copy-start | bytes 23592964
  220.9 3.6 %copy-start.14 = (f32[1024]{0:T(1024)S(1)}, f32[1024]{0:T(1024)}, u32[]{:S(2)}) copy-start(f32[1024]{0:T(1024)} %get-tuple-element.21) | copy-start | bytes 12292
  261.2 4.4 %copy-start.6 = (bf16[1024,256]{1,0:T(8,128)(2,1)S(1)}, bf16[1024,256]{1,0:T(8,128)(2,1)}, u32[]{:S(2)}) copy-start(bf16[1024,256]{1,0:T(8,128)(2,1)} %fusion.79) | copy-start | bytes 1572868
where the time goes:
time: 272 us; the launch traced here: 271 us
  waiting for transfers between devices  72.8 us (27%)
  matrix products  69.7 us (26%)
  blocking collectives  40.7 us (15%)
  local copies, waits for them, and re-layouts  32.6 us (12%)
  other arithmetic  25.7 us (9%)
  between operations  15.9 us (6%)
  starting transfers between devices  13.2 us (5%)
    ppermute x4, waiting for transfers between devices, swapped(): return lax.ppermute(value, axis, pairs)  72.8 us
    dot_general x12, matrix products, per_device(): jnp.dot(kernel_block, rows_block[:, feat_width:], preferred_element_type=...  48.3 us
    all_gather x1, blocking collectives, per_device(): lax.all_gather(jnp.concatenate([quarter_skel, quarter_coords], axis=1), '...  31.8 us
    gather x1, local copies, waits for them, and re-layouts, per_device(): jnp.take_along_axis(leaf_points, leaf_skeleton[:, :, None], axis=1)  12.4 us
    concatenate x1, other arithmetic, with_halo(): array = jnp.concatenate([before, array, after], axis=dim)  10.8 us
    unnamed x43, local copies, waits for them, and re-layouts  9.47 us
    all_gather x1, blocking collectives, per_device(): coordinates = lax.all_gather(points, 'cols', axis=1, tiled=True)  8.95 us
    ppermute x4, starting transfers between devices, swapped(): return lax.ppermute(value, axis, pairs)  6.97 us
  transfers between devices with their start and end apart: 6, of which 4 were waited for; matrix products, arithmetic and copies ran while one was open for 16% of the time, Pallas kernels for 0%

commit v1 on v0

v1 whole, which is shorter than its diff:
```python
import functools
import math

import jax
import jax.numpy as jnp
from jax import lax
from jax.experimental import pallas as pl
from jax.experimental.pallas import tpu as pltpu
from jax.sharding import PartitionSpec as P

LEAF = 1024
CHILDREN = 4
SHARPNESS = 2.0
F32 = jnp.float32
BF16 = jnp.bfloat16
VMEM_LIMIT = 48 << 20


def mm(a, b):
    return jnp.dot(a, b, preferred_element_type=F32)


def mm_t(a, b):
    return lax.dot_general(a, b, (((0,), (0,)), ((), ())), preferred_element_type=F32)


def augmented(coords, left):
    wide = coords.astype(F32)
    half = -0.5 * jnp.sum(wide * wide, axis=0, keepdims=True)
    high = half.astype(BF16).astype(F32)
    rest = half - high
    mid = rest.astype(BF16).astype(F32)
    low = rest - mid
    row = lax.broadcasted_iota(jnp.int32, coords.shape, 0)
    at, ones = (0, 3) if left else (3, 0)
    extra = jnp.where((row >= ones) & (row < ones + 3), 1.0, 0.0)
    for k, piece in enumerate((high, mid, low)):
        extra = jnp.where(row == at + k, piece, extra)
    return jnp.concatenate([coords, extra.astype(BF16)], axis=0)


def kernel_of(inner, feat):
    return jnp.exp2(inner * (2.0 * SHARPNESS / feat * math.log2(math.e))).astype(BF16)


def pick(coords, index_row, offset=0):
    n = coords.shape[1]
    place = lax.broadcasted_iota(jnp.int32, (n, index_row.shape[1]), 0)
    hot = jnp.where(place == index_row - offset, 1.0, 0.0).astype(BF16)
    return mm(coords, hot)


def leaf_kernel(pts_ref, w_ref, basis_ref, dev_ref, lskel_ref, dskel_ref, field_ref, packed_ref, skel_ref):
    feat = pts_ref.shape[0]
    leaves, rank = lskel_ref.shape
    coords = []
    for l in range(leaves):
        skel_ref[pl.ds(l * rank, rank), :] = mm(
            basis_ref[pl.ds(l * rank, rank), :], w_ref[pl.ds(l * LEAF, LEAF), :]
        ).astype(BF16)
        coords.append(pick(pts_ref[:, pl.ds(l * LEAF, LEAF)], lskel_ref[pl.ds(l, 1), :]).astype(BF16))
    packed_ref[:rank, :] = mm(dev_ref[...], skel_ref[...]).astype(BF16)
    packed_ref[rank:, :] = pick(jnp.concatenate(coords, axis=1), dskel_ref[...]).astype(BF16)
    rights = [augmented(c, False) for c in coords]
    for l in range(leaves):
        left = augmented(coords[l], True).T
        total = None
        for o in range(leaves):
            if o != l:
                term = mm(kernel_of(mm(left, rights[o]), feat), skel_ref[pl.ds(o * rank, rank), :])
                total = term if total is None else total + term
        field_ref[pl.ds(l * rank, rank), :] = total


def node_kernel(pos_ref, *refs):
    packs = refs[:CHILDREN]
    transfers = refs[CHILDREN : 2 * CHILDREN]
    gskel_ref, field_ref, group_ref = refs[2 * CHILDREN :]
    member = lax.rem(pos_ref[0], CHILDREN)
    group = pos_ref[0] // CHILDREN
    rank = field_ref.shape[0]
    feat = packs[0].shape[0] - rank
    quarter = transfers[0].shape[0]
    children = [member ^ f for f in range(CHILDREN)]
    for q in range(CHILDREN):
        total = None
        for f in range(CHILDREN):
            cols = pl.ds(pl.multiple_of(children[f] * rank, rank), rank)
            term = mm(transfers[q][:, cols], packs[f][:rank, :])
            total = term if total is None else total + term
        group_ref[pl.ds(pl.multiple_of(children[q] * quarter, quarter), quarter), :] = total.astype(BF16)
    chosen = gskel_ref[pl.ds(group, 1), :]
    coords = None
    for f in range(CHILDREN):
        term = pick(packs[f][rank:, :], chosen, children[f] * rank)
        coords = term if coords is None else coords + term
    group_ref[rank:, :] = coords.astype(BF16)
    left = augmented(packs[0][rank:, :], True).T
    total = None
    for f in range(1, CHILDREN):
        term = mm(kernel_of(mm(left, augmented(packs[f][rank:, :], False)), feat), packs[f][:rank, :])
        total = term if total is None else total + term
    field_ref[...] = total


def top_kernel(others, pos_ref, *refs):
    own_ref = refs[0]
    other_refs = refs[1 : 1 + others]
    transfers = refs[1 + others : 1 + others + CHILDREN]
    nfield_ref, lfield_ref, dev_ref, out_ref, top_ref = refs[1 + others + CHILDREN :]
    rank = nfield_ref.shape[0]
    feat = own_ref.shape[0] - rank
    quarter = transfers[0].shape[0]
    member = lax.rem(pos_ref[0], CHILDREN)
    left = augmented(own_ref[rank:, :], True).T
    total = jnp.zeros(nfield_ref.shape, F32)
    for ref in other_refs:
        total += mm(kernel_of(mm(left, augmented(ref[rank:, :], False)), feat), ref[:rank, :])
    top_ref[...] = total.astype(BF16)
    shares = nfield_ref[...]
    cols = pl.ds(pl.multiple_of(member * rank, rank), rank)
    for f in range(CHILDREN):
        rows = pl.ds(pl.multiple_of((member ^ f) * quarter, quarter), quarter)
        shares += mm_t(transfers[f][:, cols], top_ref[rows, :])
    node_total = shares.astype(BF16)
    out_ref[...] = (lfield_ref[...] + mm_t(dev_ref[...], node_total)).astype(BF16)


def near_kernel(first, far, info_ref, count_ref, list_ref, *refs):
    refs = list(refs)
    own_ref, pts_ref = refs[:2]
    w_refs = refs[2 : 2 + info_ref.shape[0] - 1]
    refs = refs[2 + len(w_refs) :]
    acc_ref = None if first else refs.pop(0)
    if far:
        basis_ref, total_ref = refs.pop(0), refs.pop(0)
    out_ref, left_ref = refs
    leaf = pl.program_id(0)
    feat = own_ref.shape[0]
    slots = list_ref.shape[1]
    chunk = 256
    per = w_refs[0].shape[0] // LEAF
    left_ref[...] = augmented(own_ref[...], True).T
    if first:
        out_ref[...] = jnp.zeros_like(out_ref)
    elif far:
        out_ref[...] = acc_ref[...] + mm_t(basis_ref[...], total_ref[...])
    else:
        out_ref[...] = acc_ref[...]
    for slot in range(slots):
        source = list_ref[leaf, slot]
        for part, w_ref in enumerate(w_refs):
            place = source - info_ref[part]

            @pl.when((slot < count_ref[leaf]) & (place >= 0) & (place < per))
            def _():
                at = pl.multiple_of((part * per + place) * LEAF, LEAF)
                right = augmented(pts_ref[:, pl.ds(at, LEAF)], False)
                rows = pl.ds(pl.multiple_of(place * LEAF, LEAF), LEAF)
                for r in range(0, LEAF, chunk):
                    block = kernel_of(mm(left_ref[pl.ds(r, chunk), :], right), feat)
                    out_ref[pl.ds(r, chunk), :] += mm(block, w_ref[rows, :])


def whole():
    return pl.BlockSpec(memory_space=pltpu.VMEM)


def scalar():
    return pl.BlockSpec(memory_space=pltpu.SMEM)


def cost(flops, nbytes):
    return pl.CostEstimate(flops=int(flops), bytes_accessed=int(nbytes), transcendentals=0)


def near_call(info, near_count, near_list, own_pts, pts, parts, acc, basis, total, pairs):
    feat, rows = own_pts.shape
    width = parts[0].shape[1]
    leaves = rows // LEAF
    const = lambda l, *_: (0, 0)
    args = [own_pts, pts, *parts]
    specs = [pl.BlockSpec((feat, LEAF), lambda l, *_: (0, l)), pl.BlockSpec(pts.shape, const)]
    specs += [pl.BlockSpec(p.shape, const) for p in parts]
    alias = {}
    if acc is not None:
        alias = {3 + len(args): 0}
        args.append(acc)
        specs.append(pl.BlockSpec((LEAF, width), lambda l, *_: (l, 0)))
    if basis is not None:
        rank = basis.shape[0] // leaves
        args += [basis, total]
        specs += [
            pl.BlockSpec((rank, LEAF), lambda l, *_: (l, 0)),
            pl.BlockSpec((rank, width), lambda l, *_: (l, 0)),
        ]
    return pl.pallas_call(
        functools.partial(near_kernel, acc is None, basis is not None),
        grid_spec=pltpu.PrefetchScalarGridSpec(
            num_scalar_prefetch=3,
            grid=(leaves,),
            in_specs=specs,
            out_specs=pl.BlockSpec((LEAF, width), lambda l, *_: (l, 0)),
            scratch_shapes=[pltpu.VMEM((LEAF, 2 * feat), BF16)],
        ),
        out_shape=jax.ShapeDtypeStruct((rows, width), F32),
        input_output_aliases=alias,
        compiler_params=pltpu.CompilerParams(vmem_limit_bytes=VMEM_LIMIT),
        cost_estimate=cost(pairs * 1.8e9, 8 << 20),
    )(info, near_count, near_list, *args)


def per_device(
    points,
    weights,
    leaf_basis,
    dev_transfer,
    group_transfer,
    leaf_skeleton,
    dev_skeleton,
    group_skeleton,
    near_list,
    near_count,
):
    size = lax.axis_size("leaf")
    position = lax.axis_index("leaf")
    rows, width = weights.shape
    leaves = rows // LEAF
    rank = leaf_skeleton.shape[1]
    groups = size // CHILDREN

    def flipped(value, mask):
        return lax.ppermute(value, "leaf", [(i, i ^ mask) for i in range(size)])

    def relayed(value):
        pairs = [(i, i + 2) for i in range(0, size - 2, 2)]
        pairs += [(i, i - 2) for i in range(3, size, 2)]
        return lax.ppermute(value, "leaf", pairs)

    own_slice = points.T
    own_pts = lax.all_gather(own_slice, "cols", axis=0, tiled=True)
    swap_slice = flipped(own_slice, 1)
    relay_slice = relayed(swap_slice)
    transfers = [group_transfer] + [flipped(group_transfer, f) for f in range(1, CHILDREN)]
    halves = 2
    step = rows // halves
    swap_w = [flipped(weights[h * step : (h + 1) * step], 1) for h in range(halves)]
    relay_w = [relayed(part) for part in swap_w]
    swap_pts = lax.all_gather(swap_slice, "cols", axis=0, tiled=True)
    relay_pts = lax.all_gather(relay_slice, "cols", axis=0, tiled=True)

    feat = own_pts.shape[0]
    params = pltpu.CompilerParams(vmem_limit_bytes=VMEM_LIMIT)
    leaf_field, packed = pl.pallas_call(
        leaf_kernel,
        out_shape=(
            jax.ShapeDtypeStruct((leaves * rank, width), F32),
            jax.ShapeDtypeStruct((rank + feat, width), BF16),
        ),
        in_specs=[whole()] * 6,
        out_specs=(whole(), whole()),
        scratch_shapes=[pltpu.VMEM((leaves * rank, width), BF16)],
        compiler_params=params,
        cost_estimate=cost(5e9, 6 << 20),
    )(own_pts, weights, leaf_basis, dev_transfer, leaf_skeleton, dev_skeleton)
    packs = [packed] + [flipped(packed, f) for f in range(1, CHILDREN)]
    pos = position.astype(jnp.int32)[None]
    node_field, group = pl.pallas_call(
        node_kernel,
        out_shape=(
            jax.ShapeDtypeStruct((rank, width), F32),
            jax.ShapeDtypeStruct((rank + feat, width), BF16),
        ),
        in_specs=[scalar()] + [whole()] * (2 * CHILDREN + 1),
        out_specs=(whole(), whole()),
        compiler_params=params,
        cost_estimate=cost(2e9, 2 << 20),
    )(pos, *packs, *transfers, group_skeleton)
    others = [
        lax.ppermute(group, "leaf", [(i, (i + CHILDREN * k) % size) for i in range(size)])
        for k in range(1, groups)
    ]
    leaf_total = pl.pallas_call(
        functools.partial(top_kernel, len(others)),
        out_shape=jax.ShapeDtypeStruct((leaves * rank, width), BF16),
        in_specs=[scalar()] + [whole()] * (len(others) + CHILDREN + 4),
        out_specs=whole(),
        scratch_shapes=[pltpu.VMEM((rank, width), BF16)],
        compiler_params=params,
        cost_estimate=cost(2e9, 3 << 20),
    )(pos, group, *others, *transfers, node_field, leaf_field, dev_transfer)

    per = leaves // halves
    counts = near_count.astype(jnp.int32)
    edges = jnp.arange(halves + 1, dtype=jnp.int32) * per
    beyond = jnp.where(position % 2 == 0, position - 1, position + 1)
    near = functools.partial(near_call, near_count=counts, near_list=near_list, own_pts=own_pts)
    own_edges = jnp.arange(2, dtype=jnp.int32) * leaves
    acc = near(own_edges + position * leaves, pts=own_pts, parts=[weights], acc=None, basis=None, total=None, pairs=6)
    acc = near(edges + (position ^ 1) * leaves, pts=swap_pts, parts=swap_w, acc=acc, basis=None, total=None, pairs=2)
    return near(
        edges + beyond * leaves,
        pts=relay_pts,
        parts=relay_w,
        acc=acc,
        basis=leaf_basis,
        total=leaf_total,
        pairs=2,
    )


def solution(mesh):
    in_specs = (
        P("leaf", "cols"),
        P("leaf", "cols"),
        P("leaf", None),
        P("leaf", None),
        P("leaf", None),
        P("leaf", None),
        P("leaf", None),
        P(),
        P("leaf", None),
        P("leaf"),
    )
    out_specs = P("leaf", "cols")
    return jax.shard_map(
        per_device, mesh=mesh, in_specs=in_specs, out_specs=out_specs, check_vma=False
    )
```

time: 272 us -> 145 us (0.53)
  the two profiles are of different devices: /device:TPU:0 before, /device:TPU:17 now
where the time goes in v1:
time: 145 us; the launch traced here: 144 us
  waiting for transfers between devices  53.4 us (37%)
  Pallas kernels  35.2 us (24%)
  blocking collectives  34.5 us (24%)
  starting transfers between devices  17.1 us (12%)
  local copies, waits for them, and re-layouts  4.03 us (3%)
    ppermute x3, waiting for transfers between devices, relayed(): return lax.ppermute(value, 'leaf', pairs)  29 us
    pallas_call x3, Pallas kernels, near_call(): pl.pallas_call(functools.partial(near_kernel, acc is None, basis is not N...  27.2 us
    ppermute x9, waiting for transfers between devices, flipped(): return lax.ppermute(value, 'leaf', [(i, i ^ mask) for i in range(size)])  24.4 us
    all_gather x1, blocking collectives, per_device(): relay_pts = lax.all_gather(relay_slice, 'cols', axis=0, tiled=True)  15 us
    all_gather x1, blocking collectives, per_device(): swap_pts = lax.all_gather(swap_slice, 'cols', axis=0, tiled=True)  10.4 us
    all_gather x1, blocking collectives, per_device(): own_pts = lax.all_gather(own_slice, 'cols', axis=0, tiled=True)  9.07 us
    ppermute x9, starting transfers between devices, flipped(): return lax.ppermute(value, 'leaf', [(i, i ^ mask) for i in range(size)])  8.24 us
    ppermute x3, starting transfers between devices, relayed(): return lax.ppermute(value, 'leaf', pairs)  5.92 us
  transfers between devices with their start and end apart: 13, of which 2 were waited for; matrix products, arithmetic and copies ran while one was open for 2% of the time, Pallas kernels for 19%

profile of v1, /device:TPU:17, one launch (start us, length us, event | category | flops | bytes accessed | tf_op | source)
XLA Modules:
  0.0 144.5 jit_solution(10396922546391564684)
XLA Ops:
  0.0 0.0 copy-start.3
  0.0 1.4 collective-permute-start.10
  1.4 1.1 collective-permute-start.11
  2.5 0.2 collective-permute-start.9
  2.7 3.0 %fusion.2 = (bf16[2048,256]{1,0:T(8,128)(2,1)}, bf16[2048,256]{1,0:T(8,128)(2,1)}) fusion(bf16[4096,256]{1,0:T(8,128)(2,1)} %w_ref.1), kind=kLoop, calls=%fused_computation.4 | loop fusion | bytes 4194304 | tf_op jit(solution)/shard_map/slice | solution.py:247
  5.7 1.2 collective-permute-start.2
  6.9 0.2 collective-permute-start.4
  7.2 0.0 copy-done.11
  7.2 9.1 %all_gather.9.refs_0_.refs_1_.pts_ref = bf16[64,4096]{1,0:T(8,128)(2,1)S(1)} all-gather(bf16[16,4096]{1,0:T(8,128)(2,1)S(1)} %bitcast.3), channel_id=1, replica_groups=mesh['leaf'=8,'cols'=4] {'cols'}, dimensions={0}, use_global_device_ids=true | all-gather | bytes 655360 | tf_op jit(solution)/shard_map/all_gather | solution.py:241
  16.2 0.0 copy-done
  16.3 0.0 copy-start.4
  16.3 0.0 copy-start.6
  16.3 0.0 copy-start.8
  16.3 9.3 %shard_map.100.refs_4_ = f32[4096,256]{1,0:T(8,128)} custom-call(s32[2]{0:T(128)S(1)} %multiply_add_fusion.info_ref, s32[4]{0:T(128)S(1)} %copy-done.3, s32[4,3]{1,0:T(4,128)S(1)} %copy-done.2, bf16[64,4096]{1,0:T(8,128)(2,1)S(1)} %all_gather.9.refs_0_.refs_1_.pts_ref, bf16[64,4096]{1,0:T(8,128)(2,1)S(1)} %all_gather.9.refs_0_.refs_1_.pts_ref, ...), custom_call_target="tpu_custom_call" | custom-call | flops 10800000000 | bytes 8388608 | tf_op jit(solution)/shard_map/pallas_call | solution.py:197
  25.6 0.0 copy-done.6
  25.6 0.0 copy-start.5
  25.7 0.0 copy-start.7
  25.7 3.9 %shard_map.102 = (f32[1024,256]{1,0:T(8,128)S(1)}, bf16[320,256]{1,0:T(8,128)(2,1)S(1)}) custom-call(bf16[64,4096]{1,0:T(8,128)(2,1)S(1)} %all_gather.9.refs_0_.refs_1_.pts_ref, bf16[4096,256]{1,0:T(8,128)(2,1)S(1)} %copy-done, bf16[1024,1024]{1,0:T(8,128)(2,1)} %refs_5_.1, bf16[256,1024]{1,0:T(8,128)(2,1)S(1)} %copy-done.4, s32[4,256]{1,0:T(4,128)S(1)} %copy-done.6, ...), custom_call_target="tpu_custom_call" | custom-call | flops 5000000000 | bytes 6291456 | tf_op jit(solution)/shard_map/pallas_call | solution.py:254
  29.5 1.0 copy-done.9
  30.5 0.0 collective-permute-done.10.refs_6_.refs_4_
  30.5 1.2 collective-permute-start
  31.8 0.0 collective-permute-done.11.refs_7_.refs_5_
  31.8 0.3 collective-permute-start.6
  32.1 0.0 collective-permute-done.9.refs_5_.refs_3_
  32.1 1.3 collective-permute-start.7
  33.4 24.4 %collective-permute-done = bf16[16,4096]{1,0:T(8,128)(2,1)S(1)} collective-permute-done((bf16[16,4096]{1,0:T(8,128)(2,1)}, bf16[16,4096]{1,0:T(8,128)(2,1)S(1)}, u32[]{:S(2)}, u32[]{:S(2)}) %collective-permute-start) | collective-permute-done | bytes 131104 | tf_op jit(solution)/shard_map/ppermute | solution.py:233
  57.8 1.2 collective-permute-start.8
  59.0 0.0 collective-permute-done.2.refs_2_
  59.0 2.0 %collective-permute-start.3 = (bf16[2048,256]{1,0:T(8,128)(2,1)}, bf16[2048,256]{1,0:T(8,128)(2,1)S(1)}, u32[]{:S(2)}, u32[]{:S(2)}) collective-permute-start(bf16[2048,256]{1,0:T(8,128)(2,1)} %collective-permute-done.2.refs_2_), channel_id=1, source_target_pairs={{0,8},{8,16},{16,24},{12,4},{20,12},{28,20},{1,9},{9,17},{17,25},{... | collective-permute-start | bytes 3145736 | tf_op jit(solution)/shard_map/ppermute | solution.py:238
  61.0 0.0 collective-permute-done.4.refs_3_
  61.0 1.9 %collective-permute-start.5 = (bf16[2048,256]{1,0:T(8,128)(2,1)}, bf16[2048,256]{1,0:T(8,128)(2,1)S(1)}, u32[]{:S(2)}, u32[]{:S(2)}) collective-permute-start(bf16[2048,256]{1,0:T(8,128)(2,1)} %collective-permute-done.4.refs_3_), channel_id=1, source_target_pairs={{0,8},{8,16},{16,24},{12,4},{20,12},{28,20},{1,9},{9,17},{17,25},{... | collective-permute-start | bytes 3145736 | tf_op jit(solution)/shard_map/ppermute | solution.py:238
  62.9 10.4 %all_gather.11.refs_1_ = bf16[64,4096]{1,0:T(8,128)(2,1)S(1)} all-gather(bf16[16,4096]{1,0:T(8,128)(2,1)S(1)} %collective-permute-done), channel_id=1, replica_groups=mesh['leaf'=8,'cols'=4] {'cols'}, dimensions={0}, use_global_device_ids=true | all-gather | bytes 655360 | tf_op jit(solution)/shard_map/all_gather | solution.py:249
  73.3 0.0 collective-permute-done.6.refs_1_
  73.3 2.0 %collective-permute-start.1 = (bf16[16,4096]{1,0:T(8,128)(2,1)S(1)}, bf16[16,4096]{1,0:T(8,128)(2,1)S(1)}, u32[]{:S(2)}, u32[]{:S(2)}) collective-permute-start(bf16[16,4096]{1,0:T(8,128)(2,1)S(1)} %collective-permute-done), channel_id=1, source_target_pairs={{0,8},{8,16},{16,24},{12,4},{20,12},{28,20},{1,9},{9,17},{17,25},{... | collective-permute-start | bytes 393224 | tf_op jit(solution)/shard_map/ppermute | solution.py:238
  75.4 0.0 collective-permute-done.7.refs_2_
  75.4 0.0 collective-permute-done.8.refs_3_
  75.4 2.0 %shard_map.103 = (f32[256,256]{1,0:T(8,128)S(1)}, bf16[320,256]{1,0:T(8,128)(2,1)S(1)}) custom-call(s32[1]{0:T(128)} %bitcast.1.pos_ref, bf16[320,256]{1,0:T(8,128)(2,1)S(1)} %get-tuple-element.9.refs_0_, bf16[320,256]{1,0:T(8,128)(2,1)S(1)} %collective-permute-done.6.refs_1_, bf16[320,256]{1,0:T(8,128)(2,1)S(1)} %collective-permute-done.7.refs_2_, ...), custom_call_target="tpu_custom_call" | custom-call | flops 2000000000 | bytes 2097152 | tf_op jit(solution)/shard_map/pallas_call | solution.py:268
  77.4 3.0 %collective-permute-start.12 = (bf16[320,256]{1,0:T(8,128)(2,1)S(1)}, bf16[320,256]{1,0:T(8,128)(2,1)S(1)}, u32[]{:S(2)}, u32[]{:S(2)}) collective-permute-start(bf16[320,256]{1,0:T(8,128)(2,1)S(1)} %get-tuple-element.10.refs_0_), channel_id=1, source_target_pairs={{0,16},{4,20},{8,24},{12,28},{16,0},{20,4},{24,8},{28,12},{1,17},{... | collective-permute-start | bytes 491528 | tf_op jit(solution)/shard_map/ppermute | solution.py:280
  80.4 29.0 %collective-permute-done.1 = bf16[16,4096]{1,0:T(8,128)(2,1)S(1)} collective-permute-done((bf16[16,4096]{1,0:T(8,128)(2,1)S(1)}, bf16[16,4096]{1,0:T(8,128)(2,1)S(1)}, u32[]{:S(2)}, u32[]{:S(2)}) %collective-permute-start.1) | collective-permute-done | bytes 131104 | tf_op jit(solution)/shard_map/ppermute | solution.py:238
  109.4 15.0 %all_gather.10.refs_1_ = bf16[64,4096]{1,0:T(8,128)(2,1)S(1)} all-gather(bf16[16,4096]{1,0:T(8,128)(2,1)S(1)} %collective-permute-done.1), channel_id=1, replica_groups=mesh['leaf'=8,'cols'=4] {'cols'}, dimensions={0}, use_global_device_ids=true | all-gather | bytes 655360 | tf_op jit(solution)/shard_map/all_gather | solution.py:250
  124.4 0.0 collective-permute-done.12.refs_1_
  124.4 0.0 copy-done.10
  124.4 2.2 %shard_map.104.refs_6_ = bf16[1024,256]{1,0:T(8,128)(2,1)S(1)} custom-call(s32[1]{0:T(128)} %bitcast.1.pos_ref, bf16[320,256]{1,0:T(8,128)(2,1)S(1)} %get-tuple-element.10.refs_0_, bf16[320,256]{1,0:T(8,128)(2,1)S(1)} %collective-permute-done.12.refs_1_, bf16[64,1024]{1,0:T(8,128)(2,1)S(1)} %copy-done.5, ...), custom_call_target="tpu_custom_call" | custom-call | flops 2000000000 | bytes 3145728 | tf_op jit(solution)/shard_map/pallas_call | solution.py:283
  126.6 0.0 copy-start.1
  126.6 10.2 %shard_map.101.refs_4_ = f32[4096,256]{1,0:T(8,128)} custom-call(s32[3]{0:T(128)S(1)} %fusion.info_ref, s32[4]{0:T(128)S(1)} %copy-done.3, s32[4,3]{1,0:T(4,128)S(1)} %copy-done.2, bf16[64,4096]{1,0:T(8,128)(2,1)S(1)} %all_gather.9.refs_0_.refs_1_.pts_ref, bf16[64,4096]{1,0:T(8,128)(2,1)S(1)} %all_gather.11.refs_1_, ...), custom_call_target="tpu_custom_call", output_to_operand_aliasing={{}: (7, {})} | custom-call | flops 3600000000 | bytes 8388608 | tf_op jit(solution)/shard_map/pallas_call | solution.py:197
  136.8 0.0 collective-permute-done.3.refs_2_
  136.8 0.0 collective-permute-done.5.refs_3_
  136.8 7.7 %shard_map.105 = f32[4096,256]{1,0:T(8,128)} custom-call(s32[3]{0:T(128)S(1)} %fusion.1.info_ref, s32[4]{0:T(128)S(1)} %copy-done.3, s32[4,3]{1,0:T(4,128)S(1)} %copy-done.2, bf16[64,4096]{1,0:T(8,128)(2,1)S(1)} %all_gather.9.refs_0_.refs_1_.pts_ref, bf16[64,4096]{1,0:T(8,128)(2,1)S(1)} %all_gather.10.refs_1_, ...), custom_call_target="tpu_custom_call", output_to_operand_aliasing={{}: (7, {})} | custom-call | flops 3600000000 | bytes 8388608 | tf_op jit(solution)/shard_map/pallas_call | solution.py:197
  (15 shorter events, 0.0 us)
Async XLA Ops:
  0.0 16.3 %copy-start = (bf16[4096,256]{1,0:T(8,128)(2,1)S(1)}, bf16[4096,256]{1,0:T(8,128)(2,1)}, u32[]{:S(2)}) copy-start(bf16[4096,256]{1,0:T(8,128)(2,1)} %w_ref.1) | copy-start | bytes 6291460
  0.0 7.2 %copy-start.11 = (bf16[4096,16]{0,1:T(8,128)(2,1)S(1)}, bf16[4096,16]{0,1:T(8,128)(2,1)}, u32[]{:S(2)}) copy-start(bf16[4096,16]{0,1:T(8,128)(2,1)} %param.10) | copy-start | bytes 393220
  0.0 16.2 %copy-start.2 = (s32[4,3]{1,0:T(4,128)S(1)}, s32[4,3]{1,0:T(4,128)}, u32[]{:S(2)}) copy-start(s32[4,3]{1,0:T(4,128)} %list_ref.5) | copy-start | bytes 148
  0.0 16.2 %copy-start.3 = (s32[4]{0:T(128)S(1)}, s32[4]{0:T(128)}, u32[]{:S(2)}) copy-start(s32[4]{0:T(128)} %count_ref.5) | copy-start | bytes 52
  0.0 30.5 %collective-permute-start.10 = (bf16[64,1024]{1,0:T(8,128)(2,1)}, bf16[64,1024]{1,0:T(8,128)(2,1)}, u32[]{:S(2)}, u32[]{:S(2)}) collective-permute-start(bf16[64,1024]{1,0:T(8,128)(2,1)} %refs_2_.3), channel_id=1, source_target_pairs={{0,8},{4,12},{8,0},{12,4},{16,24},{20,28},{24,16},{28,20},{1,9},{5... | collective-permute-start | bytes 393224 | tf_op jit(solution)/shard_map/ppermute | solution.py:233
  1.4 30.4 %collective-permute-start.11 = (bf16[64,1024]{1,0:T(8,128)(2,1)}, bf16[64,1024]{1,0:T(8,128)(2,1)}, u32[]{:S(2)}, u32[]{:S(2)}) collective-permute-start(bf16[64,1024]{1,0:T(8,128)(2,1)} %refs_2_.3), channel_id=1, source_target_pairs={{0,12},{4,8},{8,4},{12,0},{16,28},{20,24},{24,20},{28,16},{1,13},{... | collective-permute-start | bytes 393224 | tf_op jit(solution)/shard_map/ppermute | solution.py:233
  2.5 29.6 %collective-permute-start.9 = (bf16[64,1024]{1,0:T(8,128)(2,1)}, bf16[64,1024]{1,0:T(8,128)(2,1)}, u32[]{:S(2)}, u32[]{:S(2)}) collective-permute-start(bf16[64,1024]{1,0:T(8,128)(2,1)} %refs_2_.3), channel_id=1, source_target_pairs={{0,4},{4,0},{8,12},{12,8},{16,20},{20,16},{24,28},{28,24},{1,5},{5... | collective-permute-start | bytes 393224 | tf_op jit(solution)/shard_map/ppermute | solution.py:233
  5.7 53.3 %collective-permute-start.2 = (bf16[2048,256]{1,0:T(8,128)(2,1)}, bf16[2048,256]{1,0:T(8,128)(2,1)}, u32[]{:S(2)}, u32[]{:S(2)}) collective-permute-start(bf16[2048,256]{1,0:T(8,128)(2,1)} %get-tuple-element.14), channel_id=1, source_target_pairs={{0,4},{4,0},{8,12},{12,8},{16,20},{20,16},{24,28},{28,24},{1,5},{5... | collective-permute-start | bytes 3145736 | tf_op jit(solution)/shard_map/ppermute | solution.py:233
  6.9 54.0 %collective-permute-start.4 = (bf16[2048,256]{1,0:T(8,128)(2,1)}, bf16[2048,256]{1,0:T(8,128)(2,1)}, u32[]{:S(2)}, u32[]{:S(2)}) collective-permute-start(bf16[2048,256]{1,0:T(8,128)(2,1)} %get-tuple-element.13), channel_id=1, source_target_pairs={{0,4},{4,0},{8,12},{12,8},{16,20},{20,16},{24,28},{28,24},{1,5},{5... | collective-permute-start | bytes 3145736 | tf_op jit(solution)/shard_map/ppermute | solution.py:233
  16.3 9.4 %copy-start.4 = (bf16[256,1024]{1,0:T(8,128)(2,1)S(1)}, bf16[256,1024]{1,0:T(8,128)(2,1)}, u32[]{:S(2)}) copy-start(bf16[256,1024]{1,0:T(8,128)(2,1)} %refs_8_.3) | copy-start | bytes 1572868
  16.3 9.4 %copy-start.6 = (s32[4,256]{1,0:T(4,128)S(1)}, s32[4,256]{1,0:T(4,128)}, u32[]{:S(2)}) copy-start(s32[4,256]{1,0:T(4,128)} %lskel_ref.1) | copy-start | bytes 12292
  16.3 9.4 %copy-start.8 = (s32[1,256]{1,0:T(1,128)S(1)}, s32[1,256]{1,0:T(1,128)}, u32[]{:S(2)}) copy-start(s32[1,256]{1,0:T(1,128)} %dskel_ref.1) | copy-start | bytes 3076
  25.6 49.8 %copy-start.5 = (bf16[64,1024]{1,0:T(8,128)(2,1)S(1)}, bf16[64,1024]{1,0:T(8,128)(2,1)}, u32[]{:S(2)}) copy-start(bf16[64,1024]{1,0:T(8,128)(2,1)} %refs_2_.3) | copy-start | bytes 393220
  25.7 49.8 %copy-start.7 = (s32[2,256]{1,0:T(2,128)S(1)}, s32[2,256]{1,0:T(2,128)}, u32[]{:S(2)}) copy-start(s32[2,256]{1,0:T(2,128)} %refs_8_.2) | copy-start | bytes 6148
  29.5 1.0 copy-start.9
  30.5 27.2 %collective-permute-start = (bf16[16,4096]{1,0:T(8,128)(2,1)}, bf16[16,4096]{1,0:T(8,128)(2,1)S(1)}, u32[]{:S(2)}, u32[]{:S(2)}) collective-permute-start(bf16[16,4096]{1,0:T(8,128)(2,1)} %bitcast.2), channel_id=1, source_target_pairs={{0,4},{4,0},{8,12},{12,8},{16,20},{20,16},{24,28},{28,24},{1,5},{5... | collective-permute-start | bytes 393224 | tf_op jit(solution)/shard_map/ppermute | solution.py:233
  31.8 41.6 %collective-permute-start.6 = (bf16[320,256]{1,0:T(8,128)(2,1)S(1)}, bf16[320,256]{1,0:T(8,128)(2,1)S(1)}, u32[]{:S(2)}, u32[]{:S(2)}) collective-permute-start(bf16[320,256]{1,0:T(8,128)(2,1)S(1)} %get-tuple-element.9.refs_0_), channel_id=1, source_target_pairs={{0,4},{4,0},{8,12},{12,8},{16,20},{20,16},{24,28},{28,24},{1,5},{5... | collective-permute-start | bytes 491528 | tf_op jit(solution)/shard_map/ppermute | solution.py:233
  32.1 43.3 %collective-permute-start.7 = (bf16[320,256]{1,0:T(8,128)(2,1)S(1)}, bf16[320,256]{1,0:T(8,128)(2,1)S(1)}, u32[]{:S(2)}, u32[]{:S(2)}) collective-permute-start(bf16[320,256]{1,0:T(8,128)(2,1)S(1)} %get-tuple-element.9.refs_0_), channel_id=1, source_target_pairs={{0,8},{4,12},{8,0},{12,4},{16,24},{20,28},{24,16},{28,20},{1,9},{5... | collective-permute-start | bytes 491528 | tf_op jit(solution)/shard_map/ppermute | solution.py:233
  57.8 17.6 %collective-permute-start.8 = (bf16[320,256]{1,0:T(8,128)(2,1)S(1)}, bf16[320,256]{1,0:T(8,128)(2,1)S(1)}, u32[]{:S(2)}, u32[]{:S(2)}) collective-permute-start(bf16[320,256]{1,0:T(8,128)(2,1)S(1)} %get-tuple-element.9.refs_0_), channel_id=1, source_target_pairs={{0,12},{4,8},{8,4},{12,0},{16,28},{20,24},{24,20},{28,16},{1,13},{... | collective-permute-start | bytes 491528 | tf_op jit(solution)/shard_map/ppermute | solution.py:233
  59.0 77.8 %collective-permute-start.3 = (bf16[2048,256]{1,0:T(8,128)(2,1)}, bf16[2048,256]{1,0:T(8,128)(2,1)S(1)}, u32[]{:S(2)}, u32[]{:S(2)}) collective-permute-start(bf16[2048,256]{1,0:T(8,128)(2,1)} %collective-permute-done.2.refs_2_), channel_id=1, source_target_pairs={{0,8},{8,16},{16,24},{12,4},{20,12},{28,20},{1,9},{9,17},{17,25},{... | collective-permute-start | bytes 3145736 | tf_op jit(solution)/shard_map/ppermute | solution.py:238
  61.0 75.8 %collective-permute-start.5 = (bf16[2048,256]{1,0:T(8,128)(2,1)}, bf16[2048,256]{1,0:T(8,128)(2,1)S(1)}, u32[]{:S(2)}, u32[]{:S(2)}) collective-permute-start(bf16[2048,256]{1,0:T(8,128)(2,1)} %collective-permute-done.4.refs_3_), channel_id=1, source_target_pairs={{0,8},{8,16},{16,24},{12,4},{20,12},{28,20},{1,9},{9,17},{17,25},{... | collective-permute-start | bytes 3145736 | tf_op jit(solution)/shard_map/ppermute | solution.py:238
  73.3 51.1 %copy-start.10 = (f32[1024,256]{1,0:T(8,128)S(1)}, f32[1024,256]{1,0:T(8,128)}, u32[]{:S(2)}) copy-start(f32[1024,256]{1,0:T(8,128)} %copy-done.9) | copy-start | bytes 3145732
  73.3 36.0 %collective-permute-start.1 = (bf16[16,4096]{1,0:T(8,128)(2,1)S(1)}, bf16[16,4096]{1,0:T(8,128)(2,1)S(1)}, u32[]{:S(2)}, u32[]{:S(2)}) collective-permute-start(bf16[16,4096]{1,0:T(8,128)(2,1)S(1)} %collective-permute-done), channel_id=1, source_target_pairs={{0,8},{8,16},{16,24},{12,4},{20,12},{28,20},{1,9},{9,17},{17,25},{... | collective-permute-start | bytes 393224 | tf_op jit(solution)/shard_map/ppermute | solution.py:238
  77.4 47.0 %collective-permute-start.12 = (bf16[320,256]{1,0:T(8,128)(2,1)S(1)}, bf16[320,256]{1,0:T(8,128)(2,1)S(1)}, u32[]{:S(2)}, u32[]{:S(2)}) collective-permute-start(bf16[320,256]{1,0:T(8,128)(2,1)S(1)} %get-tuple-element.10.refs_0_), channel_id=1, source_target_pairs={{0,16},{4,20},{8,24},{12,28},{16,0},{20,4},{24,8},{28,12},{1,17},{... | collective-permute-start | bytes 491528 | tf_op jit(solution)/shard_map/ppermute | solution.py:280
  126.6 10.2 %copy-start.1 = (bf16[1024,1024]{1,0:T(8,128)(2,1)S(1)}, bf16[1024,1024]{1,0:T(8,128)(2,1)}, u32[]{:S(2)}) copy-start(bf16[1024,1024]{1,0:T(8,128)(2,1)} %refs_5_.1) | copy-start | bytes 6291460

commit v2 on v1

v2 whole, which is shorter than its diff:
```python
import functools
import math

import jax
import jax.numpy as jnp
from jax import lax
from jax.experimental import pallas as pl
from jax.experimental.pallas import tpu as pltpu
from jax.sharding import PartitionSpec as P

LEAF = 1024
CHILDREN = 4
SHARPNESS = 2.0
F32 = jnp.float32
BF16 = jnp.bfloat16
VMEM_LIMIT = 48 << 20


def mm(a, b):
    return jnp.dot(a, b, preferred_element_type=F32)


def mm_t(a, b):
    return lax.dot_general(a, b, (((0,), (0,)), ((), ())), preferred_element_type=F32)


def augmented(coords, left):
    wide = coords.astype(F32)
    half = -0.5 * jnp.sum(wide * wide, axis=0, keepdims=True)
    high = half.astype(BF16).astype(F32)
    rest = half - high
    mid = rest.astype(BF16).astype(F32)
    low = rest - mid
    row = lax.broadcasted_iota(jnp.int32, coords.shape, 0)
    at, ones = (0, 3) if left else (3, 0)
    extra = jnp.where((row >= ones) & (row < ones + 3), 1.0, 0.0)
    for k, piece in enumerate((high, mid, low)):
        extra = jnp.where(row == at + k, piece, extra)
    return jnp.concatenate([coords, extra.astype(BF16)], axis=0)


def kernel_of(inner, feat):
    return jnp.exp2(inner * (2.0 * SHARPNESS / feat * math.log2(math.e))).astype(BF16)


def pick(coords, index_row, offset=0):
    n = coords.shape[1]
    place = lax.broadcasted_iota(jnp.int32, (n, index_row.shape[1]), 0)
    hot = jnp.where(place == index_row - offset, 1.0, 0.0).astype(BF16)
    return mm(coords, hot)


def leaf_kernel(
    late, pts_ref, w_ref, basis_ref, dev_ref, group_ref, lskel_ref, dskel_ref,
    field_ref, packed_ref, left_ref, *refs
):
    late_refs, skel_ref = refs[:-1], refs[-1]
    feat = pts_ref.shape[0]
    leaves, rank = lskel_ref.shape
    for ref, l in zip(late_refs, late):
        ref[...] = w_ref[pl.ds(l * LEAF, LEAF), :]
    coords = []
    for l in range(leaves):
        own = pts_ref[:, pl.ds(l * LEAF, LEAF)]
        left_ref[pl.ds(l * LEAF, LEAF), :] = augmented(own, True).T
        skel_ref[pl.ds(l * rank, rank), :] = mm(
            basis_ref[pl.ds(l * rank, rank), :], w_ref[pl.ds(l * LEAF, LEAF), :]
        ).astype(BF16)
        coords.append(pick(own, lskel_ref[pl.ds(l, 1), :]).astype(BF16))
    packed_ref[:rank, :] = mm(dev_ref[...], skel_ref[...]).astype(BF16)
    packed_ref[rank : rank + feat, :] = pick(jnp.concatenate(coords, axis=1), dskel_ref[...]).astype(BF16)
    quarter = group_ref.shape[0]
    for c in range(CHILDREN):
        packed_ref[pl.ds(rank + feat + c * quarter, quarter), :] = group_ref[:, c * rank : (c + 1) * rank]
    rights = [augmented(c, False) for c in coords]
    for l in range(leaves):
        left = augmented(coords[l], True).T
        total = None
        for o in range(leaves):
            if o != l:
                term = mm(kernel_of(mm(left, rights[o]), feat), skel_ref[pl.ds(o * rank, rank), :])
                total = term if total is None else total + term
        field_ref[pl.ds(l * rank, rank), :] = total


def transfer_block(pack, child, rank, feat):
    quarter = rank // CHILDREN
    start = rank + feat
    return pack[pl.ds(pl.multiple_of(start + child * quarter, quarter), quarter), :]


def node_kernel(feat, pos_ref, *refs):
    packs = refs[:CHILDREN]
    gskel_ref, field_ref, group_ref = refs[CHILDREN:]
    member = lax.rem(pos_ref[0], CHILDREN)
    group = pos_ref[0] // CHILDREN
    rank = field_ref.shape[0]
    quarter = rank // CHILDREN
    children = [member ^ f for f in range(CHILDREN)]
    for q in range(CHILDREN):
        total = None
        for f in range(CHILDREN):
            term = mm(transfer_block(packs[q], children[f], rank, feat), packs[f][:rank, :])
            total = term if total is None else total + term
        group_ref[pl.ds(pl.multiple_of(children[q] * quarter, quarter), quarter), :] = total.astype(BF16)
    chosen = gskel_ref[pl.ds(group, 1), :]
    coords = None
    for f in range(CHILDREN):
        term = pick(packs[f][rank : rank + feat, :], chosen, children[f] * rank)
        coords = term if coords is None else coords + term
    group_ref[rank:, :] = coords.astype(BF16)
    left = augmented(packs[0][rank : rank + feat, :], True).T
    total = None
    for f in range(1, CHILDREN):
        inner = mm(left, augmented(packs[f][rank : rank + feat, :], False))
        term = mm(kernel_of(inner, feat), packs[f][:rank, :])
        total = term if total is None else total + term
    field_ref[...] = total


def top_kernel(others, pos_ref, *refs):
    own_ref = refs[0]
    other_refs = refs[1 : 1 + others]
    packs = refs[1 + others : 1 + others + CHILDREN]
    nfield_ref, lfield_ref, dev_ref, out_ref, top_ref = refs[1 + others + CHILDREN :]
    rank = nfield_ref.shape[0]
    feat = own_ref.shape[0] - rank
    quarter = rank // CHILDREN
    member = lax.rem(pos_ref[0], CHILDREN)
    left = augmented(own_ref[rank:, :], True).T
    total = jnp.zeros(nfield_ref.shape, F32)
    for ref in other_refs:
        total += mm(kernel_of(mm(left, augmented(ref[rank:, :], False)), feat), ref[:rank, :])
    top_ref[...] = total.astype(BF16)
    shares = nfield_ref[...]
    for f in range(CHILDREN):
        rows = pl.ds(pl.multiple_of((member ^ f) * quarter, quarter), quarter)
        shares += mm_t(transfer_block(packs[f], member, rank, feat), top_ref[rows, :])
    node_total = shares.astype(BF16)
    out_ref[...] = (lfield_ref[...] + mm_t(dev_ref[...], node_total)).astype(BF16)


def near_kernel(lanes, first, far, info_ref, count_ref, list_ref, *refs):
    refs = list(refs)
    left_ref, pts_ref = refs[:2]
    w_refs = refs[2 : 2 + len(lanes)]
    refs = refs[2 + len(lanes) :]
    acc_ref = None if first else refs.pop(0)
    if far:
        basis_ref, total_ref = refs.pop(0), refs.pop(0)
    (out_ref,) = refs
    leaf = pl.program_id(0)
    feat = pts_ref.shape[0]
    chunk = 256
    if first:
        out_ref[...] = jnp.zeros_like(out_ref)
    elif far:
        out_ref[...] = acc_ref[...] + mm_t(basis_ref[...], total_ref[...])
    else:
        out_ref[...] = acc_ref[...]

    def visit(slot, carry):
        source = list_ref[leaf, slot]
        for part, (lane, w_ref) in enumerate(zip(lanes, w_refs)):
            place = source - info_ref[part]

            @pl.when((place >= 0) & (place < w_ref.shape[0] // LEAF))
            def _():
                at = pl.multiple_of(place * LEAF, LEAF)
                right = augmented(pts_ref[:, pl.ds(pl.multiple_of(lane + at, LEAF), LEAF)], False)
                rows = pl.ds(at, LEAF)
                for r in range(0, LEAF, chunk):
                    block = kernel_of(mm(left_ref[pl.ds(r, chunk), :], right), feat)
                    out_ref[pl.ds(r, chunk), :] += mm(block, w_ref[rows, :])

        return carry

    lax.fori_loop(0, count_ref[leaf], visit, 0)


def whole():
    return pl.BlockSpec(memory_space=pltpu.VMEM)


def scalar():
    return pl.BlockSpec(memory_space=pltpu.SMEM)


def cost(flops, nbytes):
    return pl.CostEstimate(flops=int(flops), bytes_accessed=int(nbytes), transcendentals=0)


def near_call(counts, near_list, left, pts, parts, acc=None, basis=None, total=None, pairs=2):
    arrays = [a for a, _, _ in parts]
    lanes = tuple(n for _, n, _ in parts)
    info = jnp.stack([base for _, _, base in parts]).astype(jnp.int32)
    rows = left.shape[0]
    width = arrays[0].shape[1]
    leaves = rows // LEAF
    const = lambda l, *_: (0, 0)
    args = [left, pts, *arrays]
    block = lambda n, m: pl.BlockSpec((n, m), lambda l, *_: (l, 0))
    specs = [block(LEAF, left.shape[1]), pl.BlockSpec(pts.shape, const)]
    specs += [pl.BlockSpec(p.shape, const) for p in arrays]
    alias = {}
    if acc is not None:
        alias = {3 + len(args): 0}
        args.append(acc)
        specs.append(block(LEAF, width))
    if basis is not None:
        rank = basis.shape[0] // leaves
        args += [basis, total]
        specs += [block(rank, LEAF), block(rank, width)]
    return pl.pallas_call(
        functools.partial(near_kernel, lanes, acc is None, basis is not None),
        grid_spec=pltpu.PrefetchScalarGridSpec(
            num_scalar_prefetch=3,
            grid=(leaves,),
            in_specs=specs,
            out_specs=block(LEAF, width),
        ),
        out_shape=jax.ShapeDtypeStruct((rows, width), F32),
        input_output_aliases=alias,
        compiler_params=pltpu.CompilerParams(vmem_limit_bytes=VMEM_LIMIT),
        cost_estimate=cost(pairs * 1.8e9, 8 << 20),
    )(info, counts, near_list, *args)


def per_device(
    points,
    weights,
    leaf_basis,
    dev_transfer,
    group_transfer,
    leaf_skeleton,
    dev_skeleton,
    group_skeleton,
    near_list,
    near_count,
):
    size = lax.axis_size("leaf")
    position = lax.axis_index("leaf")
    rows, width = weights.shape
    leaves = rows // LEAF
    rank = leaf_skeleton.shape[1]
    groups = size // CHILDREN

    def flipped(value, mask):
        return lax.ppermute(value, "leaf", [(i, i ^ mask) for i in range(size)])

    def relayed(value):
        pairs = [(i, i + 2) for i in range(0, size - 2, 2)]
        pairs += [(i, i - 2) for i in range(3, size, 2)]
        return lax.ppermute(value, "leaf", pairs)

    own_slice = points.T
    swap_slice = flipped(own_slice, 1)
    relay_slice = relayed(swap_slice)
    pts = lax.all_gather(
        jnp.concatenate([own_slice, swap_slice, relay_slice], axis=1), "cols", axis=0, tiled=True
    )
    early = range(leaves // 2)
    late = range(leaves // 2, leaves)
    swap_w = [flipped(weights[l * LEAF : (l + 1) * LEAF], 1) for l in early]
    feat = pts.shape[0]
    params = pltpu.CompilerParams(vmem_limit_bytes=VMEM_LIMIT)
    pack_rows = rank + feat + CHILDREN * group_transfer.shape[0]
    leaf_field, packed, left, *late_w = pl.pallas_call(
        functools.partial(leaf_kernel, tuple(late)),
        out_shape=(
            jax.ShapeDtypeStruct((leaves * rank, width), F32),
            jax.ShapeDtypeStruct((pack_rows, width), BF16),
            jax.ShapeDtypeStruct((rows, 2 * feat), BF16),
        )
        + tuple(jax.ShapeDtypeStruct((LEAF, width), BF16) for _ in late),
        in_specs=[whole()] * 7,
        out_specs=(whole(),) * (3 + len(late)),
        scratch_shapes=[pltpu.VMEM((leaves * rank, width), BF16)],
        compiler_params=params,
        cost_estimate=cost(5e9, 6 << 20),
    )(pts, weights, leaf_basis, dev_transfer, group_transfer, leaf_skeleton, dev_skeleton)
    packs = [packed] + [flipped(packed, f) for f in range(1, CHILDREN)]
    swap_w += [flipped(part, 1) for part in late_w]
    relay_w = [relayed(part) for part in swap_w]

    pos = position.astype(jnp.int32)[None]
    node_field, group = pl.pallas_call(
        functools.partial(node_kernel, feat),
        out_shape=(
            jax.ShapeDtypeStruct((rank, width), F32),
            jax.ShapeDtypeStruct((rank + feat, width), BF16),
        ),
        in_specs=[scalar()] + [whole()] * (CHILDREN + 1),
        out_specs=(whole(), whole()),
        compiler_params=params,
        cost_estimate=cost(2e9, 2 << 20),
    )(pos, *packs, group_skeleton)
    others = [
        lax.ppermute(group, "leaf", [(i, (i + CHILDREN * k) % size) for i in range(size)])
        for k in range(1, groups)
    ]
    leaf_total = pl.pallas_call(
        functools.partial(top_kernel, len(others)),
        out_shape=jax.ShapeDtypeStruct((leaves * rank, width), BF16),
        in_specs=[scalar()] + [whole()] * (len(others) + CHILDREN + 4),
        out_specs=whole(),
        scratch_shapes=[pltpu.VMEM((rank, width), BF16)],
        compiler_params=params,
        cost_estimate=cost(2e9, 3 << 20),
    )(pos, group, *others, *packs, node_field, leaf_field, dev_transfer)

    counts = near_count.astype(jnp.int32)
    beyond = jnp.where(position % 2 == 0, position - 1, position + 1)
    own_part = [(weights, 0, position * leaves)]
    swap_parts = [(w, rows + l * LEAF, (position ^ 1) * leaves + l) for l, w in enumerate(swap_w)]
    relay_parts = [(w, 2 * rows + l * LEAF, beyond * leaves + l) for l, w in enumerate(relay_w)]
    near = functools.partial(near_call, counts, near_list, left, pts)
    half = leaves // 2
    acc = near(own_part + swap_parts[:half], pairs=7)
    acc = near(
        swap_parts[half:] + relay_parts[:half], acc=acc, basis=leaf_basis, total=leaf_total, pairs=5
    )
    return near(relay_parts[half:], acc=acc, pairs=2)


def solution(mesh):
    in_specs = (
        P("leaf", "cols"),
        P("leaf", "cols"),
        P("leaf", None),
        P("leaf", None),
        P("leaf", None),
        P("leaf", None),
        P("leaf", None),
        P(),
        P("leaf", None),
        P("leaf"),
    )
    out_specs = P("leaf", "cols")
    return jax.shard_map(
        per_device, mesh=mesh, in_specs=in_specs, out_specs=out_specs, check_vma=False
    )
```

time: 145 us -> 132 us (0.910); the launches traced: 144 us -> 130 us
  blocking collectives: 34.5 us -> 0 us
  between operations: 0.18 us -> 13.5 us
  waiting for transfers between devices: 53.4 us -> 57.5 us
  starting transfers between devices: 17.1 us -> 19.5 us
  Pallas kernels: 35.2 us -> 33 us
  other arithmetic: 0.01 us -> 1.93 us
    all_gather x3 -> x0, blocking collectives: 34.5 us -> none  [the longest x1 15 us: per_device(): relay_pts = lax.all_gather(relay_slice, 'cols', axis=0, tiled=True)]
    all_gather x0 -> x1, waiting for transfers between devices: none -> 18.8 us  [per_device(): lax.all_gather(jnp.concatenate([own_slice, swap_slice, relay_slice], axis...]
    ppermute x9 -> x8, waiting for transfers between devices: 24.4 us -> 9.49 us  [flipped(): return lax.ppermute(value, 'leaf', [(i, i ^ mask) for i in range(size)])]
    ppermute x1, waiting for transfers between devices: 0.01 us -> 14.9 us  [per_device(): lax.ppermute(group, 'leaf', [(i, (i + CHILDREN * k) % size) for i in rang...]
    ppermute x3 -> x5, waiting for transfers between devices: 29 us -> 14.3 us  [relayed(): return lax.ppermute(value, 'leaf', pairs)]
    ppermute x3 -> x5, starting transfers between devices: 5.92 us -> 12.2 us  [relayed(): return lax.ppermute(value, 'leaf', pairs)]
    ppermute x1, starting transfers between devices: 2.97 us -> 0.29 us  [per_device(): lax.ppermute(group, 'leaf', [(i, (i + CHILDREN * k) % size) for i in rang...]
    concatenate x0 -> x1, other arithmetic: none -> 1.71 us  [per_device(): jnp.concatenate([own_slice, swap_slice, relay_slice], axis=1)]
  transfers between devices with their start and end apart: 13 -> 15, of which waited for: 2 -> 8; matrix products, arithmetic and copies ran while one was open for 2% -> 2% of each run, Pallas kernels for 19% -> 19%
where the time goes in v2:
time: 132 us; the launch traced here: 130 us
  waiting for transfers between devices  57.5 us (44%)
  Pallas kernels  33 us (25%)
  starting transfers between devices  19.5 us (15%)
  between operations  13.5 us (10%)
  local copies, waits for them, and re-layouts  4.29 us (3%)
  other arithmetic  1.93 us (1%)
    pallas_call x3, Pallas kernels, near_call(): pl.pallas_call(functools.partial(near_kernel, lanes, acc is None, basis i...  26.4 us
    all_gather x1, waiting for transfers between devices, per_device(): lax.all_gather(jnp.concatenate([own_slice, swap_slice, relay_slice], axis...  18.8 us
    ppermute x1, waiting for transfers between devices, per_device(): lax.ppermute(group, 'leaf', [(i, (i + CHILDREN * k) % size) for i in rang...  14.9 us
    ppermute x5, waiting for transfers between devices, relayed(): return lax.ppermute(value, 'leaf', pairs)  14.3 us
    ppermute x5, starting transfers between devices, relayed(): return lax.ppermute(value, 'leaf', pairs)  12.2 us
    ppermute x8, waiting for transfers between devices, flipped(): return lax.ppermute(value, 'leaf', [(i, i ^ mask) for i in range(size)])  9.49 us
    ppermute x8, starting transfers between devices, flipped(): return lax.ppermute(value, 'leaf', [(i, i ^ mask) for i in range(size)])  6.94 us
    pallas_call x1, Pallas kernels, per_device(): pl.pallas_call(functools.partial(leaf_kernel, tuple(late)), out_shape=(ja...  4.52 us
  transfers between devices with their start and end apart: 15, of which 8 were waited for; matrix products, arithmetic and copies ran while one was open for 2% of the time, Pallas kernels for 19%

profile of v2, /device:TPU:17, one launch (start us, length us, event | category | flops | bytes accessed | tf_op | source)
XLA Modules:
  0.0 129.8 jit_solution(60747818442696248)
XLA Ops:
  6.5 0.0 all-gather.2.cloned.1.call-start
  6.6 1.3 %collective-permute-start = (bf16[16,4096]{1,0:T(8,128)(2,1)}, bf16[16,4096]{1,0:T(8,128)(2,1)S(1)}, u32[]{:S(2)}, u32[]{:S(2)}) collective-permute-start(bf16[16,4096]{1,0:T(8,128)(2,1)} %bitcast.11), channel_id=1, source_target_pairs={{0,4},{4,0},{8,12},{12,8},{16,20},{20,16},{24,28},{28,24},{1,5},{5... | collective-permute-start | bytes 393224 | tf_op jit(solution)/shard_map/ppermute | solution.py:249
  7.9 3.3 %collective-permute-done = bf16[16,4096]{1,0:T(8,128)(2,1)S(1)} collective-permute-done((bf16[16,4096]{1,0:T(8,128)(2,1)}, bf16[16,4096]{1,0:T(8,128)(2,1)S(1)}, u32[]{:S(2)}, u32[]{:S(2)}) %collective-permute-start) | collective-permute-done | bytes 131104 | tf_op jit(solution)/shard_map/ppermute | solution.py:249
  11.2 3.2 %collective-permute-start.1 = (bf16[16,4096]{1,0:T(8,128)(2,1)S(1)}, bf16[16,4096]{1,0:T(8,128)(2,1)S(1)}, u32[]{:S(2)}, u32[]{:S(2)}) collective-permute-start(bf16[16,4096]{1,0:T(8,128)(2,1)S(1)} %collective-permute-done), channel_id=1, source_target_pairs={{0,8},{8,16},{16,24},{12,4},{20,12},{28,20},{1,9},{9,17},{17,25},{... | collective-permute-start | bytes 393224 | tf_op jit(solution)/shard_map/ppermute | solution.py:254
  14.4 2.5 %collective-permute-done.1 = bf16[16,4096]{1,0:T(8,128)(2,1)S(1)} collective-permute-done((bf16[16,4096]{1,0:T(8,128)(2,1)S(1)}, bf16[16,4096]{1,0:T(8,128)(2,1)S(1)}, u32[]{:S(2)}, u32[]{:S(2)}) %collective-permute-start.1) | collective-permute-done | bytes 131104 | tf_op jit(solution)/shard_map/ppermute | solution.py:254
  16.9 1.7 %pad_maximum_fusion = bf16[16,12288]{1,0:T(8,128)(2,1)} fusion(bf16[16,4096]{1,0:T(8,128)(2,1)S(1)} %collective-permute-done.1, bf16[16,4096]{1,0:T(8,128)(2,1)S(1)} %collective-permute-done, bf16[16,4096]{1,0:T(8,128)(2,1)} %bitcast.12), kind=kLoop, calls=%fused_computation | loop fusion | flops 1179648 | bytes 786432 | tf_op jit(solution)/shard_map/concatenate | solution.py:260
  18.6 0.0 all-gather.2.cloned.1.call-update
  18.7 2.1 %fusion = (bf16[1024,256]{1,0:T(8,128)(2,1)S(1)}, bf16[1024,256]{1,0:T(8,128)(2,1)}) fusion(bf16[4096,256]{1,0:T(8,128)(2,1)} %refs_2_.1), kind=kLoop, calls=%fused_computation.4 | loop fusion | bytes 2097152 | tf_op jit(solution)/shard_map/slice | solution.py:264
  20.7 1.2 collective-permute-start.6
  22.0 0.2 collective-permute-start.8
  22.2 18.8 %all-gather.2.cloned.1.call-done.pts_ref.refs_1_ = bf16[64,12288]{1,0:T(8,128)(2,1)} async-done(((bf16[16,12288]{1,0:T(8,128)(2,1)}), bf16[64,12288]{1,0:T(8,128)(2,1)}) %all-gather.2.cloned.1.call-update) | async-done | bytes 1572880 | tf_op jit(solution)/shard_map/all_gather | solution.py:259
  41.0 0.0 copy-done.3
  41.0 1.4 %copy-done.1 = bf16[64,12288]{1,0:T(8,128)(2,1)S(1)} copy-done((bf16[64,12288]{1,0:T(8,128)(2,1)S(1)}, bf16[64,12288]{1,0:T(8,128)(2,1)}, u32[]{:S(2)}) %copy-start.1) | copy-done | bytes 1572888
  42.4 4.5 %shard_map.100 = (f32[1024,256]{1,0:T(8,128)S(1)}, bf16[576,256]{1,0:T(8,128)(2,1)S(1)}, bf16[4096,128]{1,0:T(8,128)(2,1)S(1)}, bf16[1024,256]{1,0:T(8,128)(2,1)S(1)}, bf16[1024,256]{1,0:T(8,128)(2,1)S(1)}) custom-call(bf16[64,12288]{1,0:T(8,128)(2,1)S(1)} %copy-done.1, bf16[4096,256]{1,0:T(8,128)(2,1)} %refs_2_.1, bf16[1024,1024]{1,0:T(8,128)(2,1)} %refs_7_.1, ...), custom_call_target="tpu_custom_call" | custom-call | flops 5000000000 | bytes 6291456 | tf_op jit(solution)/shard_map/pallas_call | solution.py:268
  47.0 1.3 collective-permute-start.10
  48.2 1.2 collective-permute-start.11
  49.4 0.3 collective-permute-start.12
  49.7 0.1 pad_add_fusion.info_ref
  49.7 0.1 pad_add_fusion.2.info_ref
  49.8 0.1 pad_add_fusion.1.info_ref
  49.9 0.0 collective-permute-done.6.refs_3_
  49.9 3.1 %collective-permute-start.7 = (bf16[1024,256]{1,0:T(8,128)(2,1)S(1)}, bf16[1024,256]{1,0:T(8,128)(2,1)S(1)}, u32[]{:S(2)}, u32[]{:S(2)}) collective-permute-start(bf16[1024,256]{1,0:T(8,128)(2,1)S(1)} %collective-permute-done.6.refs_3_), channel_id=1, source_target_pairs={{0,8},{8,16},{16,24},{12,4},{20,12},{28,20},{1,9},{9,17},{17,25},{... | collective-permute-start | bytes 1572872 | tf_op jit(solution)/shard_map/ppermute | solution.py:254
  53.0 0.0 collective-permute-done.8.refs_4_
  53.0 1.9 %collective-permute-start.9 = (bf16[1024,256]{1,0:T(8,128)(2,1)S(1)}, bf16[1024,256]{1,0:T(8,128)(2,1)S(1)}, u32[]{:S(2)}, u32[]{:S(2)}) collective-permute-start(bf16[1024,256]{1,0:T(8,128)(2,1)S(1)} %collective-permute-done.8.refs_4_), channel_id=1, source_target_pairs={{0,8},{8,16},{16,24},{12,4},{20,12},{28,20},{1,9},{9,17},{17,25},{... | collective-permute-start | bytes 1572872 | tf_op jit(solution)/shard_map/ppermute | solution.py:254
  55.0 0.4 collective-permute-done.10.refs_1_.refs_3_
  55.3 1.2 collective-permute-start.2
  56.5 0.0 collective-permute-done.11.refs_2_.refs_4_
  56.6 0.3 collective-permute-start.4
  56.8 5.8 %collective-permute-done.12.refs_3_.refs_5_ = bf16[576,256]{1,0:T(8,128)(2,1)S(1)} collective-permute-done((bf16[576,256]{1,0:T(8,128)(2,1)S(1)}, bf16[576,256]{1,0:T(8,128)(2,1)S(1)}, u32[]{:S(2)}, u32[]{:S(2)}) %collective-permute-start.12) | collective-permute-done | bytes 294944 | tf_op jit(solution)/shard_map/ppermute | solution.py:249
  62.6 0.0 copy-start.9
  62.6 0.9 shard_map.102
  63.5 0.3 collective-permute-start.13
  63.8 0.3 copy-done
  64.2 0.4 copy-done.2
  64.6 0.0 copy-done.7
  64.6 9.1 %shard_map.101.refs_6_ = f32[4096,256]{1,0:T(8,128)} custom-call(s32[3]{0:T(128)S(1)} %pad_add_fusion.2.info_ref, s32[4]{0:T(128)S(1)} %copy-done.9, s32[4,3]{1,0:T(4,128)S(1)} %copy-done.7, bf16[4096,128]{1,0:T(8,128)(2,1)S(1)} %get-tuple-element.12.refs_0_, bf16[64,12288]{1,0:T(8,128)(2,1)S(1)} %copy-done.2, bf16[4096,256]{1,0:T(8,128)(2,1)S(1)} %copy-done, ...), custom_call_target="tpu_custom_call" | custom-call | flops 12600000512 | bytes 8388608 | tf_op jit(solution)/shard_map/pallas_call | solution.py:214
  73.7 14.9 %collective-permute-done.13.refs_1_ = bf16[320,256]{1,0:T(8,128)(2,1)S(1)} collective-permute-done((bf16[320,256]{1,0:T(8,128)(2,1)S(1)}, bf16[320,256]{1,0:T(8,128)(2,1)S(1)}, u32[]{:S(2)}, u32[]{:S(2)}) %collective-permute-start.13) | collective-permute-done | bytes 163872 | tf_op jit(solution)/shard_map/ppermute | solution.py:299
  88.5 1.2 shard_map.103.refs_8_
  89.7 0.0 collective-permute-done.2.refs_2_
  89.7 1.9 %collective-permute-start.3 = (bf16[1024,256]{1,0:T(8,128)(2,1)S(1)}, bf16[1024,256]{1,0:T(8,128)(2,1)S(1)}, u32[]{:S(2)}, u32[]{:S(2)}) collective-permute-start(bf16[1024,256]{1,0:T(8,128)(2,1)S(1)} %collective-permute-done.2.refs_2_), channel_id=1, source_target_pairs={{0,8},{8,16},{16,24},{12,4},{20,12},{28,20},{1,9},{9,17},{17,25},{... | collective-permute-start | bytes 1572872 | tf_op jit(solution)/shard_map/ppermute | solution.py:254
  91.7 0.0 collective-permute-done.4.refs_3_
  91.7 2.1 %collective-permute-start.5 = (bf16[1024,256]{1,0:T(8,128)(2,1)S(1)}, bf16[1024,256]{1,0:T(8,128)(2,1)S(1)}, u32[]{:S(2)}, u32[]{:S(2)}) collective-permute-start(bf16[1024,256]{1,0:T(8,128)(2,1)S(1)} %collective-permute-done.4.refs_3_), channel_id=1, source_target_pairs={{0,8},{8,16},{16,24},{12,4},{20,12},{28,20},{1,9},{9,17},{17,25},{... | collective-permute-start | bytes 1572872 | tf_op jit(solution)/shard_map/ppermute | solution.py:254
  93.8 0.0 collective-permute-done.7.refs_4_
  93.8 0.0 collective-permute-done.9.refs_5_
  93.8 9.2 %shard_map.104.refs_4_ = f32[4096,256]{1,0:T(8,128)} custom-call(s32[4]{0:T(128)S(1)} %pad_add_fusion.1.info_ref, s32[4]{0:T(128)S(1)} %copy-done.9, s32[4,3]{1,0:T(4,128)S(1)} %copy-done.7, bf16[4096,128]{1,0:T(8,128)(2,1)S(1)} %get-tuple-element.12.refs_0_, bf16[64,12288]{1,0:T(8,128)(2,1)S(1)} %copy-done.2, ...), custom_call_target="tpu_custom_call", output_to_operand_aliasing={{}: (9, {})} | custom-call | flops 8999999488 | bytes 8388608 | tf_op jit(solution)/shard_map/pallas_call | solution.py:214
  103.0 0.6 collective-permute-done.3.refs_2_
  103.6 11.2 %collective-permute-done.5.refs_3_ = bf16[1024,256]{1,0:T(8,128)(2,1)S(1)} collective-permute-done((bf16[1024,256]{1,0:T(8,128)(2,1)S(1)}, bf16[1024,256]{1,0:T(8,128)(2,1)S(1)}, u32[]{:S(2)}, u32[]{:S(2)}) %collective-permute-start.5) | collective-permute-done | bytes 524320 | tf_op jit(solution)/shard_map/ppermute | solution.py:254
  114.9 8.1 %shard_map.105 = f32[4096,256]{1,0:T(8,128)} custom-call(s32[2]{0:T(128)S(1)} %pad_add_fusion.info_ref, s32[4]{0:T(128)S(1)} %copy-done.9, s32[4,3]{1,0:T(4,128)S(1)} %copy-done.7, bf16[4096,128]{1,0:T(8,128)(2,1)S(1)} %get-tuple-element.12.refs_0_, bf16[64,12288]{1,0:T(8,128)(2,1)S(1)} %copy-done.2, ...), custom_call_target="tpu_custom_call", output_to_operand_aliasing={{}: (7, {})} | custom-call | flops 3600000000 | bytes 8388608 | tf_op jit(solution)/shard_map/pallas_call | solution.py:214
  (14 shorter events, 0.0 us)
Async XLA Ops:
  6.5 34.5 %copy-start.3 = (bf16[256,1024]{1,0:T(8,128)(2,1)S(1)}, bf16[256,1024]{1,0:T(8,128)(2,1)}, u32[]{:S(2)}) copy-start(bf16[256,1024]{1,0:T(8,128)(2,1)} %refs_8_.1) | copy-start | bytes 1572868
  6.5 34.5 %copy-start.4 = (bf16[64,1024]{1,0:T(8,128)(2,1)S(1)}, bf16[64,1024]{1,0:T(8,128)(2,1)}, u32[]{:S(2)}) copy-start(bf16[64,1024]{1,0:T(8,128)(2,1)} %group_ref.1) | copy-start | bytes 393220
  6.5 34.5 %copy-start.5 = (s32[4,256]{1,0:T(4,128)S(1)}, s32[4,256]{1,0:T(4,128)}, u32[]{:S(2)}) copy-start(s32[4,256]{1,0:T(4,128)} %lskel_ref.1) | copy-start | bytes 12292
  6.5 34.5 %copy-start.8 = (s32[1,256]{1,0:T(1,128)S(1)}, s32[1,256]{1,0:T(1,128)}, u32[]{:S(2)}) copy-start(s32[1,256]{1,0:T(1,128)} %dskel_ref.1) | copy-start | bytes 3076
  6.5 34.5 %all-gather.2.cloned.1.call-start = ((), (), s32[]{:S(2)}) async-start(), calls=%async_computation | async-start | bytes 1966080 | tf_op jit(solution)/shard_map/all_gather | solution.py:259
  6.6 4.6 %collective-permute-start = (bf16[16,4096]{1,0:T(8,128)(2,1)}, bf16[16,4096]{1,0:T(8,128)(2,1)S(1)}, u32[]{:S(2)}, u32[]{:S(2)}) collective-permute-start(bf16[16,4096]{1,0:T(8,128)(2,1)} %bitcast.11), channel_id=1, source_target_pairs={{0,4},{4,0},{8,12},{12,8},{16,20},{20,16},{24,28},{28,24},{1,5},{5... | collective-permute-start | bytes 393224 | tf_op jit(solution)/shard_map/ppermute | solution.py:249
  11.2 5.7 %collective-permute-start.1 = (bf16[16,4096]{1,0:T(8,128)(2,1)S(1)}, bf16[16,4096]{1,0:T(8,128)(2,1)S(1)}, u32[]{:S(2)}, u32[]{:S(2)}) collective-permute-start(bf16[16,4096]{1,0:T(8,128)(2,1)S(1)} %collective-permute-done), channel_id=1, source_target_pairs={{0,8},{8,16},{16,24},{12,4},{20,12},{28,20},{1,9},{9,17},{17,25},{... | collective-permute-start | bytes 393224 | tf_op jit(solution)/shard_map/ppermute | solution.py:254
  20.7 29.2 %collective-permute-start.6 = (bf16[1024,256]{1,0:T(8,128)(2,1)}, bf16[1024,256]{1,0:T(8,128)(2,1)S(1)}, u32[]{:S(2)}, u32[]{:S(2)}) collective-permute-start(bf16[1024,256]{1,0:T(8,128)(2,1)} %get-tuple-element.20), channel_id=1, source_target_pairs={{0,4},{4,0},{8,12},{12,8},{16,20},{20,16},{24,28},{28,24},{1,5},{5... | collective-permute-start | bytes 1572872 | tf_op jit(solution)/shard_map/ppermute | solution.py:249
  22.0 31.1 %collective-permute-start.8 = (bf16[1024,256]{1,0:T(8,128)(2,1)S(1)}, bf16[1024,256]{1,0:T(8,128)(2,1)S(1)}, u32[]{:S(2)}, u32[]{:S(2)}) collective-permute-start(bf16[1024,256]{1,0:T(8,128)(2,1)S(1)} %get-tuple-element.19), channel_id=1, source_target_pairs={{0,4},{4,0},{8,12},{12,8},{16,20},{20,16},{24,28},{28,24},{1,5},{5... | collective-permute-start | bytes 1572872 | tf_op jit(solution)/shard_map/ppermute | solution.py:249
  41.0 1.4 %copy-start.1 = (bf16[64,12288]{1,0:T(8,128)(2,1)S(1)}, bf16[64,12288]{1,0:T(8,128)(2,1)}, u32[]{:S(2)}) copy-start(bf16[64,12288]{1,0:T(8,128)(2,1)} %all-gather.2.cloned.1.call-done.pts_ref.refs_1_) | copy-start | bytes 4718596
  42.4 20.1 %copy-start.6 = (s32[2,256]{1,0:T(2,128)S(1)}, s32[2,256]{1,0:T(2,128)}, u32[]{:S(2)}) copy-start(s32[2,256]{1,0:T(2,128)} %refs_4_.1) | copy-start | bytes 6148
  47.0 8.4 %collective-permute-start.10 = (bf16[576,256]{1,0:T(8,128)(2,1)S(1)}, bf16[576,256]{1,0:T(8,128)(2,1)S(1)}, u32[]{:S(2)}, u32[]{:S(2)}) collective-permute-start(bf16[576,256]{1,0:T(8,128)(2,1)S(1)} %get-tuple-element.15.refs_0_.refs_2_), channel_id=1, source_target_pairs={{0,4},{4,0},{8,12},{12,8},{16,20},{20,16},{24,28},{28,24},{1,5},{5... | collective-permute-start | bytes 884744 | tf_op jit(solution)/shard_map/ppermute | solution.py:249
  48.2 8.3 %collective-permute-start.11 = (bf16[576,256]{1,0:T(8,128)(2,1)S(1)}, bf16[576,256]{1,0:T(8,128)(2,1)S(1)}, u32[]{:S(2)}, u32[]{:S(2)}) collective-permute-start(bf16[576,256]{1,0:T(8,128)(2,1)S(1)} %get-tuple-element.15.refs_0_.refs_2_), channel_id=1, source_target_pairs={{0,8},{4,12},{8,0},{12,4},{16,24},{20,28},{24,16},{28,20},{1,9},{5... | collective-permute-start | bytes 884744 | tf_op jit(solution)/shard_map/ppermute | solution.py:249
  49.4 13.2 %collective-permute-start.12 = (bf16[576,256]{1,0:T(8,128)(2,1)S(1)}, bf16[576,256]{1,0:T(8,128)(2,1)S(1)}, u32[]{:S(2)}, u32[]{:S(2)}) collective-permute-start(bf16[576,256]{1,0:T(8,128)(2,1)S(1)} %get-tuple-element.15.refs_0_.refs_2_), channel_id=1, source_target_pairs={{0,12},{4,8},{8,4},{12,0},{16,28},{20,24},{24,20},{28,16},{1,13},{... | collective-permute-start | bytes 884744 | tf_op jit(solution)/shard_map/ppermute | solution.py:249
  49.9 43.9 %collective-permute-start.7 = (bf16[1024,256]{1,0:T(8,128)(2,1)S(1)}, bf16[1024,256]{1,0:T(8,128)(2,1)S(1)}, u32[]{:S(2)}, u32[]{:S(2)}) collective-permute-start(bf16[1024,256]{1,0:T(8,128)(2,1)S(1)} %collective-permute-done.6.refs_3_), channel_id=1, source_target_pairs={{0,8},{8,16},{16,24},{12,4},{20,12},{28,20},{1,9},{9,17},{17,25},{... | collective-permute-start | bytes 1572872 | tf_op jit(solution)/shard_map/ppermute | solution.py:254
  53.0 40.8 %collective-permute-start.9 = (bf16[1024,256]{1,0:T(8,128)(2,1)S(1)}, bf16[1024,256]{1,0:T(8,128)(2,1)S(1)}, u32[]{:S(2)}, u32[]{:S(2)}) collective-permute-start(bf16[1024,256]{1,0:T(8,128)(2,1)S(1)} %collective-permute-done.8.refs_4_), channel_id=1, source_target_pairs={{0,8},{8,16},{16,24},{12,4},{20,12},{28,20},{1,9},{9,17},{17,25},{... | collective-permute-start | bytes 1572872 | tf_op jit(solution)/shard_map/ppermute | solution.py:254
  55.3 34.4 %collective-permute-start.2 = (bf16[1024,256]{1,0:T(8,128)(2,1)S(1)}, bf16[1024,256]{1,0:T(8,128)(2,1)S(1)}, u32[]{:S(2)}, u32[]{:S(2)}) collective-permute-start(bf16[1024,256]{1,0:T(8,128)(2,1)S(1)} %get-tuple-element.13), channel_id=1, source_target_pairs={{0,4},{4,0},{8,12},{12,8},{16,20},{20,16},{24,28},{28,24},{1,5},{5... | collective-permute-start | bytes 1572872 | tf_op jit(solution)/shard_map/ppermute | solution.py:249
  56.6 35.1 %collective-permute-start.4 = (bf16[1024,256]{1,0:T(8,128)(2,1)S(1)}, bf16[1024,256]{1,0:T(8,128)(2,1)S(1)}, u32[]{:S(2)}, u32[]{:S(2)}) collective-permute-start(bf16[1024,256]{1,0:T(8,128)(2,1)S(1)} %get-tuple-element.14), channel_id=1, source_target_pairs={{0,4},{4,0},{8,12},{12,8},{16,20},{20,16},{24,28},{28,24},{1,5},{5... | collective-permute-start | bytes 1572872 | tf_op jit(solution)/shard_map/ppermute | solution.py:249
  62.6 1.6 %copy-start = (bf16[4096,256]{1,0:T(8,128)(2,1)S(1)}, bf16[4096,256]{1,0:T(8,128)(2,1)}, u32[]{:S(2)}) copy-start(bf16[4096,256]{1,0:T(8,128)(2,1)} %refs_2_.1) | copy-start | bytes 6291460
  62.6 2.0 %copy-start.2 = (bf16[64,12288]{1,0:T(8,128)(2,1)S(1)}, bf16[64,12288]{1,0:T(8,128)(2,1)}, u32[]{:S(2)}) copy-start(bf16[64,12288]{1,0:T(8,128)(2,1)} %all-gather.2.cloned.1.call-done.pts_ref.refs_1_) | copy-start | bytes 4718596
  62.6 2.0 %copy-start.7 = (s32[4,3]{1,0:T(4,128)S(1)}, s32[4,3]{1,0:T(4,128)}, u32[]{:S(2)}) copy-start(s32[4,3]{1,0:T(4,128)} %list_ref.5) | copy-start | bytes 148
  62.6 2.0 %copy-start.9 = (s32[4]{0:T(128)S(1)}, s32[4]{0:T(128)}, u32[]{:S(2)}) copy-start(s32[4]{0:T(128)} %count_ref.5) | copy-start | bytes 52
  63.5 25.0 %collective-permute-start.13 = (bf16[320,256]{1,0:T(8,128)(2,1)S(1)}, bf16[320,256]{1,0:T(8,128)(2,1)S(1)}, u32[]{:S(2)}, u32[]{:S(2)}) collective-permute-start(bf16[320,256]{1,0:T(8,128)(2,1)S(1)} %get-tuple-element.16.refs_0_), channel_id=1, source_target_pairs={{0,16},{4,20},{8,24},{12,28},{16,0},{20,4},{24,8},{28,12},{1,17},{... | collective-permute-start | bytes 491528 | tf_op jit(solution)/shard_map/ppermute | solution.py:299
  89.7 13.9 %collective-permute-start.3 = (bf16[1024,256]{1,0:T(8,128)(2,1)S(1)}, bf16[1024,256]{1,0:T(8,128)(2,1)S(1)}, u32[]{:S(2)}, u32[]{:S(2)}) collective-permute-start(bf16[1024,256]{1,0:T(8,128)(2,1)S(1)} %collective-permute-done.2.refs_2_), channel_id=1, source_target_pairs={{0,8},{8,16},{16,24},{12,4},{20,12},{28,20},{1,9},{9,17},{17,25},{... | collective-permute-start | bytes 1572872 | tf_op jit(solution)/shard_map/ppermute | solution.py:254
  91.7 23.2 %collective-permute-start.5 = (bf16[1024,256]{1,0:T(8,128)(2,1)S(1)}, bf16[1024,256]{1,0:T(8,128)(2,1)S(1)}, u32[]{:S(2)}, u32[]{:S(2)}) collective-permute-start(bf16[1024,256]{1,0:T(8,128)(2,1)S(1)} %collective-permute-done.4.refs_3_), channel_id=1, source_target_pairs={{0,8},{8,16},{16,24},{12,4},{20,12},{28,20},{1,9},{9,17},{17,25},{... | collective-permute-start | bytes 1572872 | tf_op jit(solution)/shard_map/ppermute | solution.py:254
Sparse Core Ops, SparseCore 0:
  18.8 22.1 all-gather.1

commit v3 on v2

--- a/solution.py
+++ b/solution.py
@@ -51,11 +51,13 @@
 
 
 def leaf_kernel(
-    late, pts_ref, w_ref, basis_ref, dev_ref, group_ref, lskel_ref, dskel_ref,
-    field_ref, packed_ref, left_ref, *refs
+    late, slices, w_ref, basis_ref, dev_ref, group_ref, lskel_ref, dskel_ref, *refs
 ):
-    late_refs, skel_ref = refs[:-1], refs[-1]
+    slice_refs = refs[:slices]
+    field_ref, packed_ref, left_ref, pts_ref = refs[slices : slices + 4]
+    late_refs, skel_ref = refs[slices + 4 : -1], refs[-1]
     feat = pts_ref.shape[0]
+    pts_ref[...] = jnp.concatenate([ref[...] for ref in slice_refs], axis=0)
     leaves, rank = lskel_ref.shape
     for ref, l in zip(late_refs, late):
         ref[...] = w_ref[pl.ds(l * LEAF, LEAF), :]
@@ -140,17 +142,19 @@
     out_ref[...] = (lfield_ref[...] + mm_t(dev_ref[...], node_total)).astype(BF16)
 
 
-def near_kernel(lanes, first, far, info_ref, count_ref, list_ref, *refs):
+def near_kernel(lanes, slices, first, far, info_ref, count_ref, list_ref, *refs):
     refs = list(refs)
-    left_ref, pts_ref = refs[:2]
-    w_refs = refs[2 : 2 + len(lanes)]
-    refs = refs[2 + len(lanes) :]
+    left_ref, own_ref = refs[:2]
+    halo_refs = refs[2 : 2 + slices]
+    refs = refs[2 + slices :]
+    w_refs = refs[: len(lanes)]
+    refs = refs[len(lanes) :]
     acc_ref = None if first else refs.pop(0)
     if far:
         basis_ref, total_ref = refs.pop(0), refs.pop(0)
     (out_ref,) = refs
     leaf = pl.program_id(0)
-    feat = pts_ref.shape[0]
+    feat = own_ref.shape[0]
     chunk = 256
     if first:
         out_ref[...] = jnp.zeros_like(out_ref)
@@ -167,7 +171,12 @@
             @pl.when((place >= 0) & (place < w_ref.shape[0] // LEAF))
             def _():
                 at = pl.multiple_of(place * LEAF, LEAF)
-                right = augmented(pts_ref[:, pl.ds(pl.multiple_of(lane + at, LEAF), LEAF)], False)
+                if lane is None:
+                    coords = own_ref[:, pl.ds(at, LEAF)]
+                else:
+                    cols = pl.ds(pl.multiple_of(lane + at, LEAF), LEAF)
+                    coords = jnp.concatenate([ref[:, cols] for ref in halo_refs], axis=0)
+                right = augmented(coords, False)
                 rows = pl.ds(at, LEAF)
                 for r in range(0, LEAF, chunk):
                     block = kernel_of(mm(left_ref[pl.ds(r, chunk), :], right), feat)
@@ -190,7 +199,7 @@
     return pl.CostEstimate(flops=int(flops), bytes_accessed=int(nbytes), transcendentals=0)
 
 
-def near_call(counts, near_list, left, pts, parts, acc=None, basis=None, total=None, pairs=2):
+def near_call(counts, near_list, left, own_pts, halo_pts, parts, acc=None, basis=None, total=None, pairs=2):
     arrays = [a for a, _, _ in parts]
     lanes = tuple(n for _, n, _ in parts)
     info = jnp.stack([base for _, _, base in parts]).astype(jnp.int32)
@@ -198,10 +207,10 @@
     width = arrays[0].shape[1]
     leaves = rows // LEAF
     const = lambda l, *_: (0, 0)
-    args = [left, pts, *arrays]
+    args = [left, own_pts, *halo_pts, *arrays]
     block = lambda n, m: pl.BlockSpec((n, m), lambda l, *_: (l, 0))
-    specs = [block(LEAF, left.shape[1]), pl.BlockSpec(pts.shape, const)]
-    specs += [pl.BlockSpec(p.shape, const) for p in arrays]
+    specs = [block(LEAF, left.shape[1])]
+    specs += [pl.BlockSpec(p.shape, const) for p in args[1:]]
     alias = {}
     if acc is not None:
         alias = {3 + len(args): 0}
@@ -212,7 +221,7 @@
         args += [basis, total]
         specs += [block(rank, LEAF), block(rank, width)]
     return pl.pallas_call(
-        functools.partial(near_kernel, lanes, acc is None, basis is not None),
+        functools.partial(near_kernel, lanes, len(halo_pts), acc is None, basis is not None),
         grid_spec=pltpu.PrefetchScalarGridSpec(
             num_scalar_prefetch=3,
             grid=(leaves,),
@@ -253,32 +262,38 @@
         pairs += [(i, i - 2) for i in range(3, size, 2)]
         return lax.ppermute(value, "leaf", pairs)
 
+    def over_cols(value):
+        count = lax.axis_size("cols")
+        return [value] + [
+            lax.ppermute(value, "cols", [(i, i ^ f) for i in range(count)]) for f in range(1, count)
+        ]
+
     own_slice = points.T
+    own_slices = over_cols(own_slice)
     swap_slice = flipped(own_slice, 1)
     relay_slice = relayed(swap_slice)
-    pts = lax.all_gather(
-        jnp.concatenate([own_slice, swap_slice, relay_slice], axis=1), "cols", axis=0, tiled=True
-    )
-    early = range(leaves // 2)
-    late = range(leaves // 2, leaves)
+    halo_pts = over_cols(jnp.concatenate([swap_slice, relay_slice], axis=1))
+    early = range(1)
+    late = range(1, leaves)
     swap_w = [flipped(weights[l * LEAF : (l + 1) * LEAF], 1) for l in early]
-    feat = pts.shape[0]
+    feat = sum(part.shape[0] for part in own_slices)
     params = pltpu.CompilerParams(vmem_limit_bytes=VMEM_LIMIT)
     pack_rows = rank + feat + CHILDREN * group_transfer.shape[0]
-    leaf_field, packed, left, *late_w = pl.pallas_call(
-        functools.partial(leaf_kernel, tuple(late)),
+    leaf_field, packed, left, own_pts, *late_w = pl.pallas_call(
+        functools.partial(leaf_kernel, tuple(late), len(own_slices)),
         out_shape=(
             jax.ShapeDtypeStruct((leaves * rank, width), F32),
             jax.ShapeDtypeStruct((pack_rows, width), BF16),
             jax.ShapeDtypeStruct((rows, 2 * feat), BF16),
+            jax.ShapeDtypeStruct((feat, rows), BF16),
         )
         + tuple(jax.ShapeDtypeStruct((LEAF, width), BF16) for _ in late),
-        in_specs=[whole()] * 7,
-        out_specs=(whole(),) * (3 + len(late)),
+        in_specs=[whole()] * (6 + len(own_slices)),
+        out_specs=(whole(),) * (4 + len(late)),
         scratch_shapes=[pltpu.VMEM((leaves * rank, width), BF16)],
         compiler_params=params,
         cost_estimate=cost(5e9, 6 << 20),
-    )(pts, weights, leaf_basis, dev_transfer, group_transfer, leaf_skeleton, dev_skeleton)
+    )(weights, leaf_basis, dev_transfer, group_transfer, leaf_skeleton, dev_skeleton, *own_slices)
     packs = [packed] + [flipped(packed, f) for f in range(1, CHILDREN)]
     swap_w += [flipped(part, 1) for part in late_w]
     relay_w = [relayed(part) for part in swap_w]
@@ -311,14 +326,14 @@
 
     counts = near_count.astype(jnp.int32)
     beyond = jnp.where(position % 2 == 0, position - 1, position + 1)
-    own_part = [(weights, 0, position * leaves)]
-    swap_parts = [(w, rows + l * LEAF, (position ^ 1) * leaves + l) for l, w in enumerate(swap_w)]
-    relay_parts = [(w, 2 * rows + l * LEAF, beyond * leaves + l) for l, w in enumerate(relay_w)]
-    near = functools.partial(near_call, counts, near_list, left, pts)
+    own_part = [(weights, None, position * leaves)]
+    swap_parts = [(w, l * LEAF, (position ^ 1) * leaves + l) for l, w in enumerate(swap_w)]
+    relay_parts = [(w, rows + l * LEAF, beyond * leaves + l) for l, w in enumerate(relay_w)]
+    near = functools.partial(near_call, counts, near_list, left, own_pts, halo_pts)
     half = leaves // 2
-    acc = near(own_part + swap_parts[:half], pairs=7)
+    acc = near(own_part + swap_parts[:1], pairs=6)
     acc = near(
-        swap_parts[half:] + relay_parts[:half], acc=acc, basis=leaf_basis, total=leaf_total, pairs=5
+        swap_parts[1:] + relay_parts[:half], acc=acc, basis=leaf_basis, total=leaf_total, pairs=5
     )
     return near(relay_parts[half:], acc=acc, pairs=2)
 

time: 132 us -> 116 us (0.88); the launches traced: 130 us -> 115 us
  between operations: 13.5 us -> 0.18 us
  waiting for transfers between devices: 57.5 us -> 47.4 us
  starting transfers between devices: 19.5 us -> 24.5 us
  local copies, waits for them, and re-layouts: 4.29 us -> 7.12 us
  Pallas kernels: 33 us -> 35.8 us
  other arithmetic: 1.93 us -> 0.15 us
    ppermute x5, waiting for transfers between devices: 14.3 us -> 34.2 us  [relayed(): return lax.ppermute(value, 'leaf', pairs)]
    all_gather x1 -> x0, waiting for transfers between devices: 18.8 us -> none  [per_device(): lax.all_gather(jnp.concatenate([own_slice, swap_slice, relay_slice], axis...]
    ppermute x1, waiting for transfers between devices: 14.9 us -> 0.01 us  [per_device(): lax.ppermute(group, 'leaf', [(i, (i + CHILDREN * k) % size) for i in rang...]
    ppermute x0 -> x6, waiting for transfers between devices: none -> 13.1 us  [over_cols(): lax.ppermute(value, 'cols', [(i, i ^ f) for i in range(count)])]
    ppermute x8, waiting for transfers between devices: 9.49 us -> 0.02 us  [flipped(): return lax.ppermute(value, 'leaf', [(i, i ^ mask) for i in range(size)])]
    ppermute x0 -> x6, starting transfers between devices: none -> 5.65 us  [over_cols(): lax.ppermute(value, 'cols', [(i, i ^ f) for i in range(count)])]
    unnamed x20 -> x21, local copies, waits for them, and re-layouts: 2.23 us -> 5.16 us
    pallas_call x4, Pallas kernels: 31 us -> 33.7 us  [the longest x3 29.1 us: near_call(): pl.pallas_call(functools.partial(near_kernel, lanes, len(halo_pts), acc i...]
  transfers between devices with their start and end apart: 15 -> 20, of which waited for: 8 -> 8; matrix products, arithmetic and copies ran while one was open for 2% -> 3% of each run, Pallas kernels for 19% -> 24%
where the time goes in v3:
time: 116 us; the launch traced here: 115 us
  waiting for transfers between devices  47.4 us (41%)
  Pallas kernels  35.8 us (31%)
  starting transfers between devices  24.5 us (21%)
  local copies, waits for them, and re-layouts  7.12 us (6%)
    ppermute x5, waiting for transfers between devices, relayed(): return lax.ppermute(value, 'leaf', pairs)  34.2 us
    pallas_call x3, Pallas kernels, near_call(): pl.pallas_call(functools.partial(near_kernel, lanes, len(halo_pts), acc i...  29.1 us
    ppermute x6, waiting for transfers between devices, over_cols(): lax.ppermute(value, 'cols', [(i, i ^ f) for i in range(count)])  13.1 us
    ppermute x5, starting transfers between devices, relayed(): return lax.ppermute(value, 'leaf', pairs)  12.5 us
    ppermute x8, starting transfers between devices, flipped(): return lax.ppermute(value, 'leaf', [(i, i ^ mask) for i in range(size)])  6.31 us
    ppermute x6, starting transfers between devices, over_cols(): lax.ppermute(value, 'cols', [(i, i ^ f) for i in range(count)])  5.65 us
    unnamed x21, local copies, waits for them, and re-layouts  5.16 us
    pallas_call x1, Pallas kernels, per_device(): pl.pallas_call(functools.partial(leaf_kernel, tuple(late), len(own_slices...  4.57 us
  transfers between devices with their start and end apart: 20, of which 8 were waited for; matrix products, arithmetic and copies ran while one was open for 3% of the time, Pallas kernels for 24%

profile of v3, /device:TPU:17, one launch (start us, length us, event | category | flops | bytes accessed | tf_op | source)
XLA Modules:
  0.0 115.2 jit_solution(12504219239527512498)
XLA Ops:
  0.0 0.7 collective-permute-start
  0.7 1.2 %collective-permute-start.1 = (bf16[16,4096]{1,0:T(8,128)(2,1)}, bf16[16,4096]{1,0:T(8,128)(2,1)S(1)}, u32[]{:S(2)}, u32[]{:S(2)}) collective-permute-start(bf16[16,4096]{1,0:T(8,128)(2,1)} %bitcast.12), channel_id=1, source_target_pairs={{0,2},{1,3},{2,0},{3,1},{4,6},{5,7},{6,4},{7,5},{8,10},{9,11},{10,... | collective-permute-start | bytes 393224 | tf_op jit(solution)/shard_map/ppermute | solution.py:268
  1.9 0.4 collective-permute-start.2
  2.3 1.2 %collective-permute-start.3 = (bf16[16,4096]{1,0:T(8,128)(2,1)}, bf16[16,4096]{1,0:T(8,128)(2,1)}, u32[]{:S(2)}, u32[]{:S(2)}) collective-permute-start(bf16[16,4096]{1,0:T(8,128)(2,1)} %bitcast.14), channel_id=1, source_target_pairs={{0,4},{4,0},{8,12},{12,8},{16,20},{20,16},{24,28},{28,24},{1,5},{5... | collective-permute-start | bytes 393224 | tf_op jit(solution)/shard_map/ppermute | solution.py:258
  3.6 1.9 %slice.3 = bf16[1024,256]{1,0:T(8,128)(2,1)} slice(bf16[4096,256]{1,0:T(8,128)(2,1)} %refs_6_.1), slice={[0:1024], [0:256]} | slice | bytes 1048576 | tf_op jit(solution)/shard_map/slice | solution.py:278
  5.4 0.2 collective-permute-start.13
  5.6 0.1 stack.44.info_ref
  5.7 0.1 pad_add_fusion.1.info_ref
  5.8 0.0 collective-permute-done.refs_1_
  5.8 0.3 collective-permute-done.1.refs_2_
  6.1 2.8 %collective-permute-done.2.refs_3_ = bf16[16,4096]{1,0:T(8,128)(2,1)S(1)} collective-permute-done((bf16[16,4096]{1,0:T(8,128)(2,1)}, bf16[16,4096]{1,0:T(8,128)(2,1)S(1)}, u32[]{:S(2)}, u32[]{:S(2)}) %collective-permute-start.2) | collective-permute-done | bytes 131104 | tf_op jit(solution)/shard_map/ppermute | solution.py:268
  8.9 1.0 copy-done.1
  10.0 0.9 copy-done.3
  10.9 0.9 copy-done.4
  11.8 0.7 copy-done.5
  12.5 0.7 copy-done.8
  13.1 4.6 %shard_map.100 = (f32[1024,256]{1,0:T(8,128)S(1)}, bf16[576,256]{1,0:T(8,128)(2,1)S(1)}, bf16[4096,128]{1,0:T(8,128)(2,1)S(1)}, bf16[64,4096]{1,0:T(8,128)(2,1)S...) custom-call(bf16[4096,256]{1,0:T(8,128)(2,1)} %refs_6_.1, ...), custom_call_target="tpu_custom_call" | custom-call | flops 5000000000 | bytes 6291456 | tf_op jit(solution)/shard_map/pallas_call | solution.py:282
  17.7 0.0 copy-start.7
  17.7 0.0 copy-start.9
  17.7 1.6 %collective-permute-start.16 = (bf16[576,256]{1,0:T(8,128)(2,1)S(1)}, bf16[576,256]{1,0:T(8,128)(2,1)S(1)}, u32[]{:S(2)}, u32[]{:S(2)}) collective-permute-start(bf16[576,256]{1,0:T(8,128)(2,1)S(1)} %get-tuple-element.19.refs_0_.refs_2_), channel_id=1, source_target_pairs={{0,4},{4,0},{8,12},{12,8},{16,20},{20,16},{24,28},{28,24},{1,5},{5... | collective-permute-start | bytes 884744 | tf_op jit(solution)/shard_map/ppermute | solution.py:258
  19.3 1.3 %collective-permute-start.17 = (bf16[576,256]{1,0:T(8,128)(2,1)S(1)}, bf16[576,256]{1,0:T(8,128)(2,1)S(1)}, u32[]{:S(2)}, u32[]{:S(2)}) collective-permute-start(bf16[576,256]{1,0:T(8,128)(2,1)S(1)} %get-tuple-element.19.refs_0_.refs_2_), channel_id=1, source_target_pairs={{0,8},{4,12},{8,0},{12,4},{16,24},{20,28},{24,16},{28,20},{1,9},{5... | collective-permute-start | bytes 884744 | tf_op jit(solution)/shard_map/ppermute | solution.py:258
  20.6 0.0 collective-permute-start.18
  20.6 3.2 %collective-permute-start.4 = (bf16[16,4096]{1,0:T(8,128)(2,1)}, bf16[16,4096]{1,0:T(8,128)(2,1)S(1)}, u32[]{:S(2)}, u32[]{:S(2)}) collective-permute-start(bf16[16,4096]{1,0:T(8,128)(2,1)} %collective-permute-done.3), channel_id=1, source_target_pairs={{0,8},{8,16},{16,24},{12,4},{20,12},{28,20},{1,9},{9,17},{17,25},{... | collective-permute-start | bytes 393224 | tf_op jit(solution)/shard_map/ppermute | solution.py:263
  23.8 0.9 constant_dynamic-update-slice_fusion.1
  24.7 11.3 %collective-permute-done.4 = bf16[16,4096]{1,0:T(8,128)(2,1)S(1)} collective-permute-done((bf16[16,4096]{1,0:T(8,128)(2,1)}, bf16[16,4096]{1,0:T(8,128)(2,1)S(1)}, u32[]{:S(2)}, u32[]{:S(2)}) %collective-permute-start.4) | collective-permute-done | bytes 131104 | tf_op jit(solution)/shard_map/ppermute | solution.py:263
  36.0 0.7 collective-permute-start.12
  36.7 1.6 %collective-permute-start.5 = (bf16[16,8192]{1,0:T(8,128)(2,1)S(1)}, bf16[16,8192]{1,0:T(8,128)(2,1)S(1)}, u32[]{:S(2)}, u32[]{:S(2)}) collective-permute-start(bf16[16,8192]{1,0:T(8,128)(2,1)S(1)} %constant_dynamic-update-slice_fusion.refs_2_), channel_id=1, source_target_pairs={{0,1},{1,0},{2,3},{3,2},{4,5},{5,4},{6,7},{7,6},{8,9},{9,8},{10,11... | collective-permute-start | bytes 786440 | tf_op jit(solution)/shard_map/ppermute | solution.py:268
  38.3 1.2 %collective-permute-start.6 = (bf16[16,8192]{1,0:T(8,128)(2,1)S(1)}, bf16[16,8192]{1,0:T(8,128)(2,1)S(1)}, u32[]{:S(2)}, u32[]{:S(2)}) collective-permute-start(bf16[16,8192]{1,0:T(8,128)(2,1)S(1)} %constant_dynamic-update-slice_fusion.refs_2_), channel_id=1, source_target_pairs={{0,2},{1,3},{2,0},{3,1},{4,6},{5,7},{6,4},{7,5},{8,10},{9,11},{10,... | collective-permute-start | bytes 786440 | tf_op jit(solution)/shard_map/ppermute | solution.py:268
  39.6 0.5 collective-permute-start.7
  40.1 0.1 pad_add_fusion.info_ref
  40.1 0.9 shard_map.102
  41.1 0.7 collective-permute-start.10
  41.7 4.5 %collective-permute-done.6.refs_4_ = bf16[16,8192]{1,0:T(8,128)(2,1)S(1)} collective-permute-done((bf16[16,8192]{1,0:T(8,128)(2,1)S(1)}, bf16[16,8192]{1,0:T(8,128)(2,1)S(1)}, u32[]{:S(2)}, u32[]{:S(2)}) %collective-permute-start.6) | collective-permute-done | bytes 262176 | tf_op jit(solution)/shard_map/ppermute | solution.py:268
  46.2 0.6 collective-permute-start.8
  46.8 5.5 %collective-permute-done.7.refs_5_ = bf16[16,8192]{1,0:T(8,128)(2,1)S(1)} collective-permute-done((bf16[16,8192]{1,0:T(8,128)(2,1)S(1)}, bf16[16,8192]{1,0:T(8,128)(2,1)S(1)}, u32[]{:S(2)}, u32[]{:S(2)}) %collective-permute-start.7) | collective-permute-done | bytes 262176 | tf_op jit(solution)/shard_map/ppermute | solution.py:268
  52.3 0.1 collective-permute-start.19
  52.4 2.8 %collective-permute-start.14 = (bf16[1024,256]{1,0:T(8,128)(2,1)S(1)}, bf16[1024,256]{1,0:T(8,128)(2,1)S(1)}, u32[]{:S(2)}, u32[]{:S(2)}) collective-permute-start(bf16[1024,256]{1,0:T(8,128)(2,1)S(1)} %collective-permute-done.13.refs_7_), channel_id=1, source_target_pairs={{0,8},{8,16},{16,24},{12,4},{20,12},{28,20},{1,9},{9,17},{17,25},{... | collective-permute-start | bytes 1572872 | tf_op jit(solution)/shard_map/ppermute | solution.py:263
  55.2 1.9 %collective-permute-start.15 = (bf16[1024,256]{1,0:T(8,128)(2,1)S(1)}, bf16[1024,256]{1,0:T(8,128)(2,1)S(1)}, u32[]{:S(2)}, u32[]{:S(2)}) collective-permute-start(bf16[1024,256]{1,0:T(8,128)(2,1)S(1)} %collective-permute-done.12.refs_6_), channel_id=1, source_target_pairs={{0,8},{8,16},{16,24},{12,4},{20,12},{28,20},{1,9},{9,17},{17,25},{... | collective-permute-start | bytes 1572872 | tf_op jit(solution)/shard_map/ppermute | solution.py:263
  57.2 0.0 copy-start.2
  57.2 11.9 %shard_map.101.refs_11_ = f32[4096,256]{1,0:T(8,128)} custom-call(s32[2]{0:T(128)S(1)} %pad_add_fusion.1.info_ref, s32[4]{0:T(128)S(1)} %copy-done.9, s32[4,3]{1,0:T(4,128)S(1)} %copy-done.7, bf16[4096,128]{1,0:T(8,128)(2,1)S(1)} %get-tuple-element.14.refs_0_, bf16[64,4096]{1,0:T(8,128)(2,1)S(1)} %get-tuple-element.15.refs_1_, ...), custom_call_target="tpu_custom_call" | custom-call | flops 10800000000 | bytes 8388608 | tf_op jit(solution)/shard_map/pallas_call | solution.py:223
  69.1 1.2 %shard_map.103.refs_13_ = bf16[1024,256]{1,0:T(8,128)(2,1)S(1)} custom-call(s32[1]{0:T(128)} %bitcast.10.pos_ref, bf16[320,256]{1,0:T(8,128)(2,1)S(1)} %get-tuple-element.20.refs_0_, bf16[320,256]{1,0:T(8,128)(2,1)S(1)} %collective-permute-done.19.refs_1_, bf16[576,256]{1,0:T(8,128)(2,1)S(1)} %get-tuple-element.19.refs_0_.refs_2_, ...), custom_call_target="tpu_custom_call" | custom-call | flops 2000000000 | bytes 3145728 | tf_op jit(solution)/shard_map/pallas_call | solution.py:317
  70.3 1.9 %collective-permute-start.11 = (bf16[1024,256]{1,0:T(8,128)(2,1)S(1)}, bf16[1024,256]{1,0:T(8,128)(2,1)S(1)}, u32[]{:S(2)}, u32[]{:S(2)}) collective-permute-start(bf16[1024,256]{1,0:T(8,128)(2,1)S(1)} %collective-permute-done.10.refs_8_), channel_id=1, source_target_pairs={{0,8},{8,16},{16,24},{12,4},{20,12},{28,20},{1,9},{9,17},{17,25},{... | collective-permute-start | bytes 1572872 | tf_op jit(solution)/shard_map/ppermute | solution.py:263
  72.2 2.7 %collective-permute-start.9 = (bf16[1024,256]{1,0:T(8,128)(2,1)S(1)}, bf16[1024,256]{1,0:T(8,128)(2,1)S(1)}, u32[]{:S(2)}, u32[]{:S(2)}) collective-permute-start(bf16[1024,256]{1,0:T(8,128)(2,1)S(1)} %collective-permute-done.8.refs_7_), channel_id=1, source_target_pairs={{0,8},{8,16},{16,24},{12,4},{20,12},{28,20},{1,9},{9,17},{17,25},{... | collective-permute-start | bytes 1572872 | tf_op jit(solution)/shard_map/ppermute | solution.py:263
  75.0 9.9 %collective-permute-done.15.refs_10_ = bf16[1024,256]{1,0:T(8,128)(2,1)S(1)} collective-permute-done((bf16[1024,256]{1,0:T(8,128)(2,1)S(1)}, bf16[1024,256]{1,0:T(8,128)(2,1)S(1)}, u32[]{:S(2)}, u32[]{:S(2)}) %collective-permute-start.15) | collective-permute-done | bytes 524320 | tf_op jit(solution)/shard_map/ppermute | solution.py:263
  84.9 9.4 %shard_map.104.refs_8_ = f32[4096,256]{1,0:T(8,128)} custom-call(s32[5]{0:T(128)S(1)} %stack.44.info_ref, s32[4]{0:T(128)S(1)} %copy-done.9, s32[4,3]{1,0:T(4,128)S(1)} %copy-done.7, bf16[4096,128]{1,0:T(8,128)(2,1)S(1)} %get-tuple-element.14.refs_0_, bf16[64,4096]{1,0:T(8,128)(2,1)S(1)} %get-tuple-element.15.refs_1_, ...), custom_call_target="tpu_custom_call", output_to_operand_aliasing={{}: (14, {})} | custom-call | flops 8999999488 | bytes 8388608 | tf_op jit(solution)/shard_map/pallas_call | solution.py:223
  94.3 1.8 %collective-permute-done.11.refs_7_ = bf16[1024,256]{1,0:T(8,128)(2,1)S(1)} collective-permute-done((bf16[1024,256]{1,0:T(8,128)(2,1)S(1)}, bf16[1024,256]{1,0:T(8,128)(2,1)S(1)}, u32[]{:S(2)}, u32[]{:S(2)}) %collective-permute-start.11) | collective-permute-done | bytes 524320 | tf_op jit(solution)/shard_map/ppermute | solution.py:263
  96.1 11.2 %collective-permute-done.9.refs_6_ = bf16[1024,256]{1,0:T(8,128)(2,1)S(1)} collective-permute-done((bf16[1024,256]{1,0:T(8,128)(2,1)S(1)}, bf16[1024,256]{1,0:T(8,128)(2,1)S(1)}, u32[]{:S(2)}, u32[]{:S(2)}) %collective-permute-start.9) | collective-permute-done | bytes 524320 | tf_op jit(solution)/shard_map/ppermute | solution.py:263
  107.3 7.8 %shard_map.105 = f32[4096,256]{1,0:T(8,128)} custom-call(s32[2]{0:T(128)S(1)} %pad_add_fusion.info_ref, s32[4]{0:T(128)S(1)} %copy-done.9, s32[4,3]{1,0:T(4,128)S(1)} %copy-done.7, bf16[4096,128]{1,0:T(8,128)(2,1)S(1)} %get-tuple-element.14.refs_0_, bf16[64,4096]{1,0:T(8,128)(2,1)S(1)} %get-tuple-element.15.refs_1_, ...), custom_call_target="tpu_custom_call", output_to_operand_aliasing={{}: (11, {})} | custom-call | flops 3600000000 | bytes 8388608 | tf_op jit(solution)/shard_map/pallas_call | solution.py:223
  (24 shorter events, 0.1 us)
Async XLA Ops:
  0.0 5.8 %collective-permute-start = (bf16[16,4096]{1,0:T(8,128)(2,1)}, bf16[16,4096]{1,0:T(8,128)(2,1)S(1)}, u32[]{:S(2)}, u32[]{:S(2)}) collective-permute-start(bf16[16,4096]{1,0:T(8,128)(2,1)} %bitcast.11), channel_id=1, source_target_pairs={{0,1},{1,0},{2,3},{3,2},{4,5},{5,4},{6,7},{7,6},{8,9},{9,8},{10,11... | collective-permute-start | bytes 393224 | tf_op jit(solution)/shard_map/ppermute | solution.py:268
  0.7 5.4 %collective-permute-start.1 = (bf16[16,4096]{1,0:T(8,128)(2,1)}, bf16[16,4096]{1,0:T(8,128)(2,1)S(1)}, u32[]{:S(2)}, u32[]{:S(2)}) collective-permute-start(bf16[16,4096]{1,0:T(8,128)(2,1)} %bitcast.12), channel_id=1, source_target_pairs={{0,2},{1,3},{2,0},{3,1},{4,6},{5,7},{6,4},{7,5},{8,10},{9,11},{10,... | collective-permute-start | bytes 393224 | tf_op jit(solution)/shard_map/ppermute | solution.py:268
  1.9 7.0 %collective-permute-start.2 = (bf16[16,4096]{1,0:T(8,128)(2,1)}, bf16[16,4096]{1,0:T(8,128)(2,1)S(1)}, u32[]{:S(2)}, u32[]{:S(2)}) collective-permute-start(bf16[16,4096]{1,0:T(8,128)(2,1)} %bitcast.13), channel_id=1, source_target_pairs={{0,3},{1,2},{2,1},{3,0},{4,7},{5,6},{6,5},{7,4},{8,11},{9,10},{10,... | collective-permute-start | bytes 393224 | tf_op jit(solution)/shard_map/ppermute | solution.py:268
  2.3 18.3 %collective-permute-start.3 = (bf16[16,4096]{1,0:T(8,128)(2,1)}, bf16[16,4096]{1,0:T(8,128)(2,1)}, u32[]{:S(2)}, u32[]{:S(2)}) collective-permute-start(bf16[16,4096]{1,0:T(8,128)(2,1)} %bitcast.14), channel_id=1, source_target_pairs={{0,4},{4,0},{8,12},{12,8},{16,20},{20,16},{24,28},{28,24},{1,5},{5... | collective-permute-start | bytes 393224 | tf_op jit(solution)/shard_map/ppermute | solution.py:258
  5.4 46.9 %collective-permute-start.13 = (bf16[1024,256]{1,0:T(8,128)(2,1)}, bf16[1024,256]{1,0:T(8,128)(2,1)S(1)}, u32[]{:S(2)}, u32[]{:S(2)}) collective-permute-start(bf16[1024,256]{1,0:T(8,128)(2,1)} %slice.3), channel_id=1, source_target_pairs={{0,4},{4,0},{8,12},{12,8},{16,20},{20,16},{24,28},{28,24},{1,5},{5... | collective-permute-start | bytes 1572872 | tf_op jit(solution)/shard_map/ppermute | solution.py:258
  5.7 34.4 %copy-start.6 = (s32[2,256]{1,0:T(2,128)S(1)}, s32[2,256]{1,0:T(2,128)}, u32[]{:S(2)}) copy-start(s32[2,256]{1,0:T(2,128)} %refs_4_.1) | copy-start | bytes 6148
  8.9 1.0 copy-start.1
  10.0 0.9 copy-start.3
  10.9 0.9 copy-start.4
  11.8 0.7 copy-start.5
  12.5 0.7 copy-start.8
  17.7 39.4 %copy-start = (bf16[4096,256]{1,0:T(8,128)(2,1)S(1)}, bf16[4096,256]{1,0:T(8,128)(2,1)}, u32[]{:S(2)}) copy-start(bf16[4096,256]{1,0:T(8,128)(2,1)} %refs_6_.1) | copy-start | bytes 6291460
  17.7 39.4 %copy-start.7 = (s32[4,3]{1,0:T(4,128)S(1)}, s32[4,3]{1,0:T(4,128)}, u32[]{:S(2)}) copy-start(s32[4,3]{1,0:T(4,128)} %list_ref.5) | copy-start | bytes 148
  17.7 39.4 %copy-start.9 = (s32[4]{0:T(128)S(1)}, s32[4]{0:T(128)}, u32[]{:S(2)}) copy-start(s32[4]{0:T(128)} %count_ref.5) | copy-start | bytes 52
  17.7 19.0 %collective-permute-start.16 = (bf16[576,256]{1,0:T(8,128)(2,1)S(1)}, bf16[576,256]{1,0:T(8,128)(2,1)S(1)}, u32[]{:S(2)}, u32[]{:S(2)}) collective-permute-start(bf16[576,256]{1,0:T(8,128)(2,1)S(1)} %get-tuple-element.19.refs_0_.refs_2_), channel_id=1, source_target_pairs={{0,4},{4,0},{8,12},{12,8},{16,20},{20,16},{24,28},{28,24},{1,5},{5... | collective-permute-start | bytes 884744 | tf_op jit(solution)/shard_map/ppermute | solution.py:258
  19.3 19.0 %collective-permute-start.17 = (bf16[576,256]{1,0:T(8,128)(2,1)S(1)}, bf16[576,256]{1,0:T(8,128)(2,1)S(1)}, u32[]{:S(2)}, u32[]{:S(2)}) collective-permute-start(bf16[576,256]{1,0:T(8,128)(2,1)S(1)} %get-tuple-element.19.refs_0_.refs_2_), channel_id=1, source_target_pairs={{0,8},{4,12},{8,0},{12,4},{16,24},{20,28},{24,16},{28,20},{1,9},{5... | collective-permute-start | bytes 884744 | tf_op jit(solution)/shard_map/ppermute | solution.py:258
  20.6 18.9 %collective-permute-start.18 = (bf16[576,256]{1,0:T(8,128)(2,1)S(1)}, bf16[576,256]{1,0:T(8,128)(2,1)S(1)}, u32[]{:S(2)}, u32[]{:S(2)}) collective-permute-start(bf16[576,256]{1,0:T(8,128)(2,1)S(1)} %get-tuple-element.19.refs_0_.refs_2_), channel_id=1, source_target_pairs={{0,12},{4,8},{8,4},{12,0},{16,28},{20,24},{24,20},{28,16},{1,13},{... | collective-permute-start | bytes 884744 | tf_op jit(solution)/shard_map/ppermute | solution.py:258
  20.6 15.3 %collective-permute-start.4 = (bf16[16,4096]{1,0:T(8,128)(2,1)}, bf16[16,4096]{1,0:T(8,128)(2,1)S(1)}, u32[]{:S(2)}, u32[]{:S(2)}) collective-permute-start(bf16[16,4096]{1,0:T(8,128)(2,1)} %collective-permute-done.3), channel_id=1, source_target_pairs={{0,8},{8,16},{16,24},{12,4},{20,12},{28,20},{1,9},{9,17},{17,25},{... | collective-permute-start | bytes 393224 | tf_op jit(solution)/shard_map/ppermute | solution.py:263
  36.0 19.2 %collective-permute-start.12 = (bf16[1024,256]{1,0:T(8,128)(2,1)S(1)}, bf16[1024,256]{1,0:T(8,128)(2,1)S(1)}, u32[]{:S(2)}, u32[]{:S(2)}) collective-permute-start(bf16[1024,256]{1,0:T(8,128)(2,1)S(1)} %get-tuple-element.18), channel_id=1, source_target_pairs={{0,4},{4,0},{8,12},{12,8},{16,20},{20,16},{24,28},{28,24},{1,5},{5... | collective-permute-start | bytes 1572872 | tf_op jit(solution)/shard_map/ppermute | solution.py:258
  36.7 4.3 %collective-permute-start.5 = (bf16[16,8192]{1,0:T(8,128)(2,1)S(1)}, bf16[16,8192]{1,0:T(8,128)(2,1)S(1)}, u32[]{:S(2)}, u32[]{:S(2)}) collective-permute-start(bf16[16,8192]{1,0:T(8,128)(2,1)S(1)} %constant_dynamic-update-slice_fusion.refs_2_), channel_id=1, source_target_pairs={{0,1},{1,0},{2,3},{3,2},{4,5},{5,4},{6,7},{7,6},{8,9},{9,8},{10,11... | collective-permute-start | bytes 786440 | tf_op jit(solution)/shard_map/ppermute | solution.py:268
  38.3 7.9 %collective-permute-start.6 = (bf16[16,8192]{1,0:T(8,128)(2,1)S(1)}, bf16[16,8192]{1,0:T(8,128)(2,1)S(1)}, u32[]{:S(2)}, u32[]{:S(2)}) collective-permute-start(bf16[16,8192]{1,0:T(8,128)(2,1)S(1)} %constant_dynamic-update-slice_fusion.refs_2_), channel_id=1, source_target_pairs={{0,2},{1,3},{2,0},{3,1},{4,6},{5,7},{6,4},{7,5},{8,10},{9,11},{10,... | collective-permute-start | bytes 786440 | tf_op jit(solution)/shard_map/ppermute | solution.py:268
  39.6 12.7 %collective-permute-start.7 = (bf16[16,8192]{1,0:T(8,128)(2,1)S(1)}, bf16[16,8192]{1,0:T(8,128)(2,1)S(1)}, u32[]{:S(2)}, u32[]{:S(2)}) collective-permute-start(bf16[16,8192]{1,0:T(8,128)(2,1)S(1)} %constant_dynamic-update-slice_fusion.refs_2_), channel_id=1, source_target_pairs={{0,3},{1,2},{2,1},{3,0},{4,7},{5,6},{6,5},{7,4},{8,11},{9,10},{10,... | collective-permute-start | bytes 786440 | tf_op jit(solution)/shard_map/ppermute | solution.py:268
  41.1 29.2 %collective-permute-start.10 = (bf16[1024,256]{1,0:T(8,128)(2,1)S(1)}, bf16[1024,256]{1,0:T(8,128)(2,1)S(1)}, u32[]{:S(2)}, u32[]{:S(2)}) collective-permute-start(bf16[1024,256]{1,0:T(8,128)(2,1)S(1)} %get-tuple-element.17), channel_id=1, source_target_pairs={{0,4},{4,0},{8,12},{12,8},{16,20},{20,16},{24,28},{28,24},{1,5},{5... | collective-permute-start | bytes 1572872 | tf_op jit(solution)/shard_map/ppermute | solution.py:258
  46.2 26.0 %collective-permute-start.8 = (bf16[1024,256]{1,0:T(8,128)(2,1)S(1)}, bf16[1024,256]{1,0:T(8,128)(2,1)S(1)}, u32[]{:S(2)}, u32[]{:S(2)}) collective-permute-start(bf16[1024,256]{1,0:T(8,128)(2,1)S(1)} %get-tuple-element.16), channel_id=1, source_target_pairs={{0,4},{4,0},{8,12},{12,8},{16,20},{20,16},{24,28},{28,24},{1,5},{5... | collective-permute-start | bytes 1572872 | tf_op jit(solution)/shard_map/ppermute | solution.py:258
  52.3 16.8 %collective-permute-start.19 = (bf16[320,256]{1,0:T(8,128)(2,1)S(1)}, bf16[320,256]{1,0:T(8,128)(2,1)S(1)}, u32[]{:S(2)}, u32[]{:S(2)}) collective-permute-start(bf16[320,256]{1,0:T(8,128)(2,1)S(1)} %get-tuple-element.20.refs_0_), channel_id=1, source_target_pairs={{0,16},{4,20},{8,24},{12,28},{16,0},{20,4},{24,8},{28,12},{1,17},{... | collective-permute-start | bytes 491528 | tf_op jit(solution)/shard_map/ppermute | solution.py:314
  52.4 22.6 %collective-permute-start.14 = (bf16[1024,256]{1,0:T(8,128)(2,1)S(1)}, bf16[1024,256]{1,0:T(8,128)(2,1)S(1)}, u32[]{:S(2)}, u32[]{:S(2)}) collective-permute-start(bf16[1024,256]{1,0:T(8,128)(2,1)S(1)} %collective-permute-done.13.refs_7_), channel_id=1, source_target_pairs={{0,8},{8,16},{16,24},{12,4},{20,12},{28,20},{1,9},{9,17},{17,25},{... | collective-permute-start | bytes 1572872 | tf_op jit(solution)/shard_map/ppermute | solution.py:263
  55.2 29.7 %collective-permute-start.15 = (bf16[1024,256]{1,0:T(8,128)(2,1)S(1)}, bf16[1024,256]{1,0:T(8,128)(2,1)S(1)}, u32[]{:S(2)}, u32[]{:S(2)}) collective-permute-start(bf16[1024,256]{1,0:T(8,128)(2,1)S(1)} %collective-permute-done.12.refs_6_), channel_id=1, source_target_pairs={{0,8},{8,16},{16,24},{12,4},{20,12},{28,20},{1,9},{9,17},{17,25},{... | collective-permute-start | bytes 1572872 | tf_op jit(solution)/shard_map/ppermute | solution.py:263
  57.2 11.9 %copy-start.2 = (bf16[256,1024]{1,0:T(8,128)(2,1)S(1)}, bf16[256,1024]{1,0:T(8,128)(2,1)}, u32[]{:S(2)}) copy-start(bf16[256,1024]{1,0:T(8,128)(2,1)} %refs_8_.1) | copy-start | bytes 1572868
  70.3 25.8 %collective-permute-start.11 = (bf16[1024,256]{1,0:T(8,128)(2,1)S(1)}, bf16[1024,256]{1,0:T(8,128)(2,1)S(1)}, u32[]{:S(2)}, u32[]{:S(2)}) collective-permute-start(bf16[1024,256]{1,0:T(8,128)(2,1)S(1)} %collective-permute-done.10.refs_8_), channel_id=1, source_target_pairs={{0,8},{8,16},{16,24},{12,4},{20,12},{28,20},{1,9},{9,17},{17,25},{... | collective-permute-start | bytes 1572872 | tf_op jit(solution)/shard_map/ppermute | solution.py:263
  72.2 35.1 %collective-permute-start.9 = (bf16[1024,256]{1,0:T(8,128)(2,1)S(1)}, bf16[1024,256]{1,0:T(8,128)(2,1)S(1)}, u32[]{:S(2)}, u32[]{:S(2)}) collective-permute-start(bf16[1024,256]{1,0:T(8,128)(2,1)S(1)} %collective-permute-done.8.refs_7_), channel_id=1, source_target_pairs={{0,8},{8,16},{16,24},{12,4},{20,12},{28,20},{1,9},{9,17},{17,25},{... | collective-permute-start | bytes 1572872 | tf_op jit(solution)/shard_map/ppermute | solution.py:263

commit v4 on v3

--- a/solution.py
+++ b/solution.py
@@ -273,8 +273,8 @@
     swap_slice = flipped(own_slice, 1)
     relay_slice = relayed(swap_slice)
     halo_pts = over_cols(jnp.concatenate([swap_slice, relay_slice], axis=1))
-    early = range(1)
-    late = range(1, leaves)
+    early = range(leaves // 2)
+    late = range(leaves // 2, leaves)
     swap_w = [flipped(weights[l * LEAF : (l + 1) * LEAF], 1) for l in early]
     feat = sum(part.shape[0] for part in own_slices)
     params = pltpu.CompilerParams(vmem_limit_bytes=VMEM_LIMIT)

time: 116 us -> 121 us (1.043); the launches traced: 115 us -> 122 us
  waiting for transfers between devices: 47.4 us -> 58.6 us
  Pallas kernels: 35.8 us -> 31.6 us
    ppermute x8, waiting for transfers between devices: 0.02 us -> 13 us  [flipped(): return lax.ppermute(value, 'leaf', [(i, i ^ mask) for i in range(size)])]
    pallas_call x3, Pallas kernels: 29.1 us -> 25 us  [near_call(): pl.pallas_call(functools.partial(near_kernel, lanes, len(halo_pts), acc i...]
    ppermute x6, waiting for transfers between devices: 13.1 us -> 11.4 us  [over_cols(): lax.ppermute(value, 'cols', [(i, i ^ f) for i in range(count)])]
    ppermute x5, starting transfers between devices: 12.5 us -> 11.2 us  [relayed(): return lax.ppermute(value, 'leaf', pairs)]
  transfers between devices with their start and end apart: 20 -> 20, of which waited for: 8 -> 9; matrix products, arithmetic and copies ran while one was open for 3% -> 3% of each run, Pallas kernels for 24% -> 19%
where the time goes in v4:
time: 121 us; the launch traced here: 122 us
  waiting for transfers between devices  58.6 us (48%)
  Pallas kernels  31.6 us (26%)
  starting transfers between devices  23.7 us (20%)
  local copies, waits for them, and re-layouts  7.32 us (6%)
    ppermute x5, waiting for transfers between devices, relayed(): return lax.ppermute(value, 'leaf', pairs)  34.2 us
    pallas_call x3, Pallas kernels, near_call(): pl.pallas_call(functools.partial(near_kernel, lanes, len(halo_pts), acc i...  25 us
    ppermute x8, waiting for transfers between devices, flipped(): return lax.ppermute(value, 'leaf', [(i, i ^ mask) for i in range(size)])  13 us
    ppermute x6, waiting for transfers between devices, over_cols(): lax.ppermute(value, 'cols', [(i, i ^ f) for i in range(count)])  11.4 us
    ppermute x5, starting transfers between devices, relayed(): return lax.ppermute(value, 'leaf', pairs)  11.2 us
    ppermute x8, starting transfers between devices, flipped(): return lax.ppermute(value, 'leaf', [(i, i ^ mask) for i in range(size)])  7.17 us
    ppermute x6, starting transfers between devices, over_cols(): lax.ppermute(value, 'cols', [(i, i ^ f) for i in range(count)])  5.31 us
    unnamed x21, local copies, waits for them, and re-layouts  5.16 us
  transfers between devices with their start and end apart: 20, of which 9 were waited for; matrix products, arithmetic and copies ran while one was open for 3% of the time, Pallas kernels for 19%

profile of v4, /device:TPU:17, one launch (start us, length us, event | category | flops | bytes accessed | tf_op | source)
XLA Modules:
  0.0 121.5 jit_solution(8149222472607861050)
XLA Ops:
  0.0 0.7 collective-permute-start
  0.7 1.2 collective-permute-start.1
  1.9 0.4 collective-permute-start.2
  2.3 1.2 %collective-permute-start.3 = (bf16[16,4096]{1,0:T(8,128)(2,1)}, bf16[16,4096]{1,0:T(8,128)(2,1)}, u32[]{:S(2)}, u32[]{:S(2)}) collective-permute-start(bf16[16,4096]{1,0:T(8,128)(2,1)} %bitcast.14), channel_id=1, source_target_pairs={{0,4},{4,0},{8,12},{12,8},{16,20},{20,16},{24,28},{28,24},{1,5},{5... | collective-permute-start | bytes 393224 | tf_op jit(solution)/shard_map/ppermute | solution.py:258
  3.6 2.1 %fusion = (bf16[1024,256]{1,0:T(8,128)(2,1)}, bf16[1024,256]{1,0:T(8,128)(2,1)S(1)}) fusion(bf16[4096,256]{1,0:T(8,128)(2,1)} %refs_6_.1), kind=kLoop, calls=%fused_computation.4 | loop fusion | bytes 2097152 | tf_op jit(solution)/shard_map/slice | solution.py:278
  5.6 0.2 collective-permute-start.13
  5.8 0.1 stack.44.info_ref
  5.9 0.1 pad_add_fusion.1.info_ref
  6.0 0.0 collective-permute-done.refs_1_
  6.0 1.2 %collective-permute-start.12 = (bf16[1024,256]{1,0:T(8,128)(2,1)S(1)}, bf16[1024,256]{1,0:T(8,128)(2,1)S(1)}, u32[]{:S(2)}, u32[]{:S(2)}) collective-permute-start(bf16[1024,256]{1,0:T(8,128)(2,1)S(1)} %get-tuple-element.22), channel_id=1, source_target_pairs={{0,4},{4,0},{8,12},{12,8},{16,20},{20,16},{24,28},{28,24},{1,5},{5... | collective-permute-start | bytes 1572872 | tf_op jit(solution)/shard_map/ppermute | solution.py:258
  7.2 1.7 %collective-permute-done.2.refs_3_ = bf16[16,4096]{1,0:T(8,128)(2,1)S(1)} collective-permute-done((bf16[16,4096]{1,0:T(8,128)(2,1)}, bf16[16,4096]{1,0:T(8,128)(2,1)S(1)}, u32[]{:S(2)}, u32[]{:S(2)}) %collective-permute-start.2) | collective-permute-done | bytes 131104 | tf_op jit(solution)/shard_map/ppermute | solution.py:268
  8.9 1.0 copy-done.1
  10.0 0.9 copy-done.3
  10.9 0.9 copy-done.4
  11.8 0.7 copy-done.5
  12.5 0.7 copy-done.8
  13.1 4.5 %shard_map.100 = (f32[1024,256]{1,0:T(8,128)S(1)}, bf16[576,256]{1,0:T(8,128)(2,1)S(1)}, bf16[4096,128]{1,0:T(8,128)(2,1)S(1)}, bf16[64,4096]{1,0:T(8,128)(2,1)S...) custom-call(bf16[4096,256]{1,0:T(8,128)(2,1)} %refs_6_.1, bf16[1024,1024]{1,0:T(8,128)(2,1)} %refs_12_.1, ...), custom_call_target="tpu_custom_call" | custom-call | flops 5000000000 | bytes 6291456 | tf_op jit(solution)/shard_map/pallas_call | solution.py:282
  17.7 0.0 copy-start.7
  17.7 0.0 copy-start.9
  17.7 1.6 %collective-permute-start.16 = (bf16[576,256]{1,0:T(8,128)(2,1)S(1)}, bf16[576,256]{1,0:T(8,128)(2,1)S(1)}, u32[]{:S(2)}, u32[]{:S(2)}) collective-permute-start(bf16[576,256]{1,0:T(8,128)(2,1)S(1)} %get-tuple-element.17.refs_0_.refs_2_), channel_id=1, source_target_pairs={{0,4},{4,0},{8,12},{12,8},{16,20},{20,16},{24,28},{28,24},{1,5},{5... | collective-permute-start | bytes 884744 | tf_op jit(solution)/shard_map/ppermute | solution.py:258
  19.3 1.3 %collective-permute-start.17 = (bf16[576,256]{1,0:T(8,128)(2,1)S(1)}, bf16[576,256]{1,0:T(8,128)(2,1)S(1)}, u32[]{:S(2)}, u32[]{:S(2)}) collective-permute-start(bf16[576,256]{1,0:T(8,128)(2,1)S(1)} %get-tuple-element.17.refs_0_.refs_2_), channel_id=1, source_target_pairs={{0,8},{4,12},{8,0},{12,4},{16,24},{20,28},{24,16},{28,20},{1,9},{5... | collective-permute-start | bytes 884744 | tf_op jit(solution)/shard_map/ppermute | solution.py:258
  20.6 2.1 %collective-permute-start.4 = (bf16[16,4096]{1,0:T(8,128)(2,1)}, bf16[16,4096]{1,0:T(8,128)(2,1)S(1)}, u32[]{:S(2)}, u32[]{:S(2)}) collective-permute-start(bf16[16,4096]{1,0:T(8,128)(2,1)} %collective-permute-done.3), channel_id=1, source_target_pairs={{0,8},{8,16},{16,24},{12,4},{20,12},{28,20},{1,9},{9,17},{17,25},{... | collective-permute-start | bytes 393224 | tf_op jit(solution)/shard_map/ppermute | solution.py:263
  22.7 0.9 constant_dynamic-update-slice_fusion.1
  23.6 6.0 %collective-permute-done.4 = bf16[16,4096]{1,0:T(8,128)(2,1)S(1)} collective-permute-done((bf16[16,4096]{1,0:T(8,128)(2,1)}, bf16[16,4096]{1,0:T(8,128)(2,1)S(1)}, u32[]{:S(2)}, u32[]{:S(2)}) %collective-permute-start.4) | collective-permute-done | bytes 131104 | tf_op jit(solution)/shard_map/ppermute | solution.py:263
  29.7 13.0 %collective-permute-done.16.refs_1_.refs_3_ = bf16[576,256]{1,0:T(8,128)(2,1)S(1)} collective-permute-done((bf16[576,256]{1,0:T(8,128)(2,1)S(1)}, bf16[576,256]{1,0:T(8,128)(2,1)S(1)}, u32[]{:S(2)}, u32[]{:S(2)}) %collective-permute-start.16) | collective-permute-done | bytes 294944 | tf_op jit(solution)/shard_map/ppermute | solution.py:258
  42.7 1.4 %collective-permute-start.5 = (bf16[16,8192]{1,0:T(8,128)(2,1)S(1)}, bf16[16,8192]{1,0:T(8,128)(2,1)S(1)}, u32[]{:S(2)}, u32[]{:S(2)}) collective-permute-start(bf16[16,8192]{1,0:T(8,128)(2,1)S(1)} %constant_dynamic-update-slice_fusion.refs_2_), channel_id=1, source_target_pairs={{0,1},{1,0},{2,3},{3,2},{4,5},{5,4},{6,7},{7,6},{8,9},{9,8},{10,11... | collective-permute-start | bytes 786440 | tf_op jit(solution)/shard_map/ppermute | solution.py:268
  44.0 1.2 collective-permute-start.6
  45.3 0.4 collective-permute-start.7
  45.7 0.1 pad_add_fusion.info_ref
  45.8 0.9 shard_map.102
  46.7 0.8 collective-permute-start.10
  47.5 4.5 %collective-permute-done.6.refs_4_ = bf16[16,8192]{1,0:T(8,128)(2,1)S(1)} collective-permute-done((bf16[16,8192]{1,0:T(8,128)(2,1)S(1)}, bf16[16,8192]{1,0:T(8,128)(2,1)S(1)}, u32[]{:S(2)}, u32[]{:S(2)}) %collective-permute-start.6) | collective-permute-done | bytes 262176 | tf_op jit(solution)/shard_map/ppermute | solution.py:268
  52.0 0.7 collective-permute-start.8
  52.7 5.3 %collective-permute-done.7.refs_5_ = bf16[16,8192]{1,0:T(8,128)(2,1)S(1)} collective-permute-done((bf16[16,8192]{1,0:T(8,128)(2,1)S(1)}, bf16[16,8192]{1,0:T(8,128)(2,1)S(1)}, u32[]{:S(2)}, u32[]{:S(2)}) %collective-permute-start.7) | collective-permute-done | bytes 262176 | tf_op jit(solution)/shard_map/ppermute | solution.py:268
  58.0 0.1 collective-permute-start.19
  58.0 3.2 %collective-permute-start.14 = (bf16[1024,256]{1,0:T(8,128)(2,1)S(1)}, bf16[1024,256]{1,0:T(8,128)(2,1)S(1)}, u32[]{:S(2)}, u32[]{:S(2)}) collective-permute-start(bf16[1024,256]{1,0:T(8,128)(2,1)S(1)} %collective-permute-done.13.refs_7_), channel_id=1, source_target_pairs={{0,8},{8,16},{16,24},{12,4},{20,12},{28,20},{1,9},{9,17},{17,25},{... | collective-permute-start | bytes 1572872 | tf_op jit(solution)/shard_map/ppermute | solution.py:263
  61.3 1.9 %collective-permute-start.15 = (bf16[1024,256]{1,0:T(8,128)(2,1)S(1)}, bf16[1024,256]{1,0:T(8,128)(2,1)S(1)}, u32[]{:S(2)}, u32[]{:S(2)}) collective-permute-start(bf16[1024,256]{1,0:T(8,128)(2,1)S(1)} %collective-permute-done.12.refs_6_), channel_id=1, source_target_pairs={{0,8},{8,16},{16,24},{12,4},{20,12},{28,20},{1,9},{9,17},{17,25},{... | collective-permute-start | bytes 1572872 | tf_op jit(solution)/shard_map/ppermute | solution.py:263
  63.2 0.0 copy-start.2
  63.2 9.0 %shard_map.101.refs_11_ = f32[4096,256]{1,0:T(8,128)} custom-call(s32[2]{0:T(128)S(1)} %pad_add_fusion.1.info_ref, s32[4]{0:T(128)S(1)} %copy-done.9, s32[4,3]{1,0:T(4,128)S(1)} %copy-done.7, bf16[4096,128]{1,0:T(8,128)(2,1)S(1)} %get-tuple-element.13.refs_0_, bf16[64,4096]{1,0:T(8,128)(2,1)S(1)} %get-tuple-element.14.refs_1_, ...), custom_call_target="tpu_custom_call" | custom-call | flops 10800000000 | bytes 8388608 | tf_op jit(solution)/shard_map/pallas_call | solution.py:223
  72.3 1.2 shard_map.103.refs_13_
  73.5 1.9 %collective-permute-start.11 = (bf16[1024,256]{1,0:T(8,128)(2,1)S(1)}, bf16[1024,256]{1,0:T(8,128)(2,1)S(1)}, u32[]{:S(2)}, u32[]{:S(2)}) collective-permute-start(bf16[1024,256]{1,0:T(8,128)(2,1)S(1)} %collective-permute-done.10.refs_8_), channel_id=1, source_target_pairs={{0,8},{8,16},{16,24},{12,4},{20,12},{28,20},{1,9},{9,17},{17,25},{... | collective-permute-start | bytes 1572872 | tf_op jit(solution)/shard_map/ppermute | solution.py:263
  75.4 2.1 %collective-permute-start.9 = (bf16[1024,256]{1,0:T(8,128)(2,1)S(1)}, bf16[1024,256]{1,0:T(8,128)(2,1)S(1)}, u32[]{:S(2)}, u32[]{:S(2)}) collective-permute-start(bf16[1024,256]{1,0:T(8,128)(2,1)S(1)} %collective-permute-done.8.refs_7_), channel_id=1, source_target_pairs={{0,8},{8,16},{16,24},{12,4},{20,12},{28,20},{1,9},{9,17},{17,25},{... | collective-permute-start | bytes 1572872 | tf_op jit(solution)/shard_map/ppermute | solution.py:263
  77.5 2.3 %collective-permute-done.14.refs_9_ = bf16[1024,256]{1,0:T(8,128)(2,1)S(1)} collective-permute-done((bf16[1024,256]{1,0:T(8,128)(2,1)S(1)}, bf16[1024,256]{1,0:T(8,128)(2,1)S(1)}, u32[]{:S(2)}, u32[]{:S(2)}) %collective-permute-start.14) | collective-permute-done | bytes 524320 | tf_op jit(solution)/shard_map/ppermute | solution.py:263
  79.9 11.2 %collective-permute-done.15.refs_10_ = bf16[1024,256]{1,0:T(8,128)(2,1)S(1)} collective-permute-done((bf16[1024,256]{1,0:T(8,128)(2,1)S(1)}, bf16[1024,256]{1,0:T(8,128)(2,1)S(1)}, u32[]{:S(2)}, u32[]{:S(2)}) %collective-permute-start.15) | collective-permute-done | bytes 524320 | tf_op jit(solution)/shard_map/ppermute | solution.py:263
  91.1 7.9 %shard_map.104.refs_8_ = f32[4096,256]{1,0:T(8,128)} custom-call(s32[5]{0:T(128)S(1)} %stack.44.info_ref, s32[4]{0:T(128)S(1)} %copy-done.9, s32[4,3]{1,0:T(4,128)S(1)} %copy-done.7, bf16[4096,128]{1,0:T(8,128)(2,1)S(1)} %get-tuple-element.13.refs_0_, bf16[64,4096]{1,0:T(8,128)(2,1)S(1)} %get-tuple-element.14.refs_1_, ...), custom_call_target="tpu_custom_call", output_to_operand_aliasing={{}: (14, {})} | custom-call | flops 8999999488 | bytes 8388608 | tf_op jit(solution)/shard_map/pallas_call | solution.py:223
  99.0 3.3 %collective-permute-done.11.refs_7_ = bf16[1024,256]{1,0:T(8,128)(2,1)S(1)} collective-permute-done((bf16[1024,256]{1,0:T(8,128)(2,1)S(1)}, bf16[1024,256]{1,0:T(8,128)(2,1)S(1)}, u32[]{:S(2)}, u32[]{:S(2)}) %collective-permute-start.11) | collective-permute-done | bytes 524320 | tf_op jit(solution)/shard_map/ppermute | solution.py:263
  102.3 11.2 %collective-permute-done.9.refs_6_ = bf16[1024,256]{1,0:T(8,128)(2,1)S(1)} collective-permute-done((bf16[1024,256]{1,0:T(8,128)(2,1)S(1)}, bf16[1024,256]{1,0:T(8,128)(2,1)S(1)}, u32[]{:S(2)}, u32[]{:S(2)}) %collective-permute-start.9) | collective-permute-done | bytes 524320 | tf_op jit(solution)/shard_map/ppermute | solution.py:263
  113.6 8.0 %shard_map.105 = f32[4096,256]{1,0:T(8,128)} custom-call(s32[2]{0:T(128)S(1)} %pad_add_fusion.info_ref, s32[4]{0:T(128)S(1)} %copy-done.9, s32[4,3]{1,0:T(4,128)S(1)} %copy-done.7, bf16[4096,128]{1,0:T(8,128)(2,1)S(1)} %get-tuple-element.13.refs_0_, bf16[64,4096]{1,0:T(8,128)(2,1)S(1)} %get-tuple-element.14.refs_1_, ...), custom_call_target="tpu_custom_call", output_to_operand_aliasing={{}: (11, {})} | custom-call | flops 3600000000 | bytes 8388608 | tf_op jit(solution)/shard_map/pallas_call | solution.py:223
  (24 shorter events, 0.1 us)
Async XLA Ops:
  0.0 6.0 %collective-permute-start = (bf16[16,4096]{1,0:T(8,128)(2,1)}, bf16[16,4096]{1,0:T(8,128)(2,1)S(1)}, u32[]{:S(2)}, u32[]{:S(2)}) collective-permute-start(bf16[16,4096]{1,0:T(8,128)(2,1)} %bitcast.11), channel_id=1, source_target_pairs={{0,1},{1,0},{2,3},{3,2},{4,5},{5,4},{6,7},{7,6},{8,9},{9,8},{10,11... | collective-permute-start | bytes 393224 | tf_op jit(solution)/shard_map/ppermute | solution.py:268
  0.7 6.6 %collective-permute-start.1 = (bf16[16,4096]{1,0:T(8,128)(2,1)}, bf16[16,4096]{1,0:T(8,128)(2,1)S(1)}, u32[]{:S(2)}, u32[]{:S(2)}) collective-permute-start(bf16[16,4096]{1,0:T(8,128)(2,1)} %bitcast.12), channel_id=1, source_target_pairs={{0,2},{1,3},{2,0},{3,1},{4,6},{5,7},{6,4},{7,5},{8,10},{9,11},{10,... | collective-permute-start | bytes 393224 | tf_op jit(solution)/shard_map/ppermute | solution.py:268
  1.9 7.0 %collective-permute-start.2 = (bf16[16,4096]{1,0:T(8,128)(2,1)}, bf16[16,4096]{1,0:T(8,128)(2,1)S(1)}, u32[]{:S(2)}, u32[]{:S(2)}) collective-permute-start(bf16[16,4096]{1,0:T(8,128)(2,1)} %bitcast.13), channel_id=1, source_target_pairs={{0,3},{1,2},{2,1},{3,0},{4,7},{5,6},{6,5},{7,4},{8,11},{9,10},{10,... | collective-permute-start | bytes 393224 | tf_op jit(solution)/shard_map/ppermute | solution.py:268
  2.3 18.3 %collective-permute-start.3 = (bf16[16,4096]{1,0:T(8,128)(2,1)}, bf16[16,4096]{1,0:T(8,128)(2,1)}, u32[]{:S(2)}, u32[]{:S(2)}) collective-permute-start(bf16[16,4096]{1,0:T(8,128)(2,1)} %bitcast.14), channel_id=1, source_target_pairs={{0,4},{4,0},{8,12},{12,8},{16,20},{20,16},{24,28},{28,24},{1,5},{5... | collective-permute-start | bytes 393224 | tf_op jit(solution)/shard_map/ppermute | solution.py:258
  5.6 52.4 %collective-permute-start.13 = (bf16[1024,256]{1,0:T(8,128)(2,1)}, bf16[1024,256]{1,0:T(8,128)(2,1)S(1)}, u32[]{:S(2)}, u32[]{:S(2)}) collective-permute-start(bf16[1024,256]{1,0:T(8,128)(2,1)} %get-tuple-element.21), channel_id=1, source_target_pairs={{0,4},{4,0},{8,12},{12,8},{16,20},{20,16},{24,28},{28,24},{1,5},{5... | collective-permute-start | bytes 1572872 | tf_op jit(solution)/shard_map/ppermute | solution.py:258
  6.0 55.2 %collective-permute-start.12 = (bf16[1024,256]{1,0:T(8,128)(2,1)S(1)}, bf16[1024,256]{1,0:T(8,128)(2,1)S(1)}, u32[]{:S(2)}, u32[]{:S(2)}) collective-permute-start(bf16[1024,256]{1,0:T(8,128)(2,1)S(1)} %get-tuple-element.22), channel_id=1, source_target_pairs={{0,4},{4,0},{8,12},{12,8},{16,20},{20,16},{24,28},{28,24},{1,5},{5... | collective-permute-start | bytes 1572872 | tf_op jit(solution)/shard_map/ppermute | solution.py:258
  8.9 1.0 copy-start.1
  10.0 0.9 copy-start.3
  10.9 0.9 copy-start.4
  11.8 0.7 copy-start.5
  12.5 0.7 copy-start.8
  13.1 32.6 %copy-start.6 = (s32[2,256]{1,0:T(2,128)S(1)}, s32[2,256]{1,0:T(2,128)}, u32[]{:S(2)}) copy-start(s32[2,256]{1,0:T(2,128)} %refs_4_.1) | copy-start | bytes 6148
  17.7 45.5 %copy-start = (bf16[4096,256]{1,0:T(8,128)(2,1)S(1)}, bf16[4096,256]{1,0:T(8,128)(2,1)}, u32[]{:S(2)}) copy-start(bf16[4096,256]{1,0:T(8,128)(2,1)} %refs_6_.1) | copy-start | bytes 6291460
  17.7 45.5 %copy-start.7 = (s32[4,3]{1,0:T(4,128)S(1)}, s32[4,3]{1,0:T(4,128)}, u32[]{:S(2)}) copy-start(s32[4,3]{1,0:T(4,128)} %list_ref.5) | copy-start | bytes 148
  17.7 45.5 %copy-start.9 = (s32[4]{0:T(128)S(1)}, s32[4]{0:T(128)}, u32[]{:S(2)}) copy-start(s32[4]{0:T(128)} %count_ref.5) | copy-start | bytes 52
  17.7 25.0 %collective-permute-start.16 = (bf16[576,256]{1,0:T(8,128)(2,1)S(1)}, bf16[576,256]{1,0:T(8,128)(2,1)S(1)}, u32[]{:S(2)}, u32[]{:S(2)}) collective-permute-start(bf16[576,256]{1,0:T(8,128)(2,1)S(1)} %get-tuple-element.17.refs_0_.refs_2_), channel_id=1, source_target_pairs={{0,4},{4,0},{8,12},{12,8},{16,20},{20,16},{24,28},{28,24},{1,5},{5... | collective-permute-start | bytes 884744 | tf_op jit(solution)/shard_map/ppermute | solution.py:258
  19.3 24.7 %collective-permute-start.17 = (bf16[576,256]{1,0:T(8,128)(2,1)S(1)}, bf16[576,256]{1,0:T(8,128)(2,1)S(1)}, u32[]{:S(2)}, u32[]{:S(2)}) collective-permute-start(bf16[576,256]{1,0:T(8,128)(2,1)S(1)} %get-tuple-element.17.refs_0_.refs_2_), channel_id=1, source_target_pairs={{0,8},{4,12},{8,0},{12,4},{16,24},{20,28},{24,16},{28,20},{1,9},{5... | collective-permute-start | bytes 884744 | tf_op jit(solution)/shard_map/ppermute | solution.py:258
  20.6 9.0 %collective-permute-start.4 = (bf16[16,4096]{1,0:T(8,128)(2,1)}, bf16[16,4096]{1,0:T(8,128)(2,1)S(1)}, u32[]{:S(2)}, u32[]{:S(2)}) collective-permute-start(bf16[16,4096]{1,0:T(8,128)(2,1)} %collective-permute-done.3), channel_id=1, source_target_pairs={{0,8},{8,16},{16,24},{12,4},{20,12},{28,20},{1,9},{9,17},{17,25},{... | collective-permute-start | bytes 393224 | tf_op jit(solution)/shard_map/ppermute | solution.py:263
  29.7 15.6 %collective-permute-start.18 = (bf16[576,256]{1,0:T(8,128)(2,1)S(1)}, bf16[576,256]{1,0:T(8,128)(2,1)S(1)}, u32[]{:S(2)}, u32[]{:S(2)}) collective-permute-start(bf16[576,256]{1,0:T(8,128)(2,1)S(1)} %get-tuple-element.17.refs_0_.refs_2_), channel_id=1, source_target_pairs={{0,12},{4,8},{8,4},{12,0},{16,28},{20,24},{24,20},{28,16},{1,13},{... | collective-permute-start | bytes 884744 | tf_op jit(solution)/shard_map/ppermute | solution.py:258
  42.7 4.0 %collective-permute-start.5 = (bf16[16,8192]{1,0:T(8,128)(2,1)S(1)}, bf16[16,8192]{1,0:T(8,128)(2,1)S(1)}, u32[]{:S(2)}, u32[]{:S(2)}) collective-permute-start(bf16[16,8192]{1,0:T(8,128)(2,1)S(1)} %constant_dynamic-update-slice_fusion.refs_2_), channel_id=1, source_target_pairs={{0,1},{1,0},{2,3},{3,2},{4,5},{5,4},{6,7},{7,6},{8,9},{9,8},{10,11... | collective-permute-start | bytes 786440 | tf_op jit(solution)/shard_map/ppermute | solution.py:268
  44.0 7.9 %collective-permute-start.6 = (bf16[16,8192]{1,0:T(8,128)(2,1)S(1)}, bf16[16,8192]{1,0:T(8,128)(2,1)S(1)}, u32[]{:S(2)}, u32[]{:S(2)}) collective-permute-start(bf16[16,8192]{1,0:T(8,128)(2,1)S(1)} %constant_dynamic-update-slice_fusion.refs_2_), channel_id=1, source_target_pairs={{0,2},{1,3},{2,0},{3,1},{4,6},{5,7},{6,4},{7,5},{8,10},{9,11},{10,... | collective-permute-start | bytes 786440 | tf_op jit(solution)/shard_map/ppermute | solution.py:268
  45.3 12.7 %collective-permute-start.7 = (bf16[16,8192]{1,0:T(8,128)(2,1)S(1)}, bf16[16,8192]{1,0:T(8,128)(2,1)S(1)}, u32[]{:S(2)}, u32[]{:S(2)}) collective-permute-start(bf16[16,8192]{1,0:T(8,128)(2,1)S(1)} %constant_dynamic-update-slice_fusion.refs_2_), channel_id=1, source_target_pairs={{0,3},{1,2},{2,1},{3,0},{4,7},{5,6},{6,5},{7,4},{8,11},{9,10},{10,... | collective-permute-start | bytes 786440 | tf_op jit(solution)/shard_map/ppermute | solution.py:268
  46.7 26.8 %collective-permute-start.10 = (bf16[1024,256]{1,0:T(8,128)(2,1)S(1)}, bf16[1024,256]{1,0:T(8,128)(2,1)S(1)}, u32[]{:S(2)}, u32[]{:S(2)}) collective-permute-start(bf16[1024,256]{1,0:T(8,128)(2,1)S(1)} %get-tuple-element.16), channel_id=1, source_target_pairs={{0,4},{4,0},{8,12},{12,8},{16,20},{20,16},{24,28},{28,24},{1,5},{5... | collective-permute-start | bytes 1572872 | tf_op jit(solution)/shard_map/ppermute | solution.py:258
  52.0 23.4 %collective-permute-start.8 = (bf16[1024,256]{1,0:T(8,128)(2,1)S(1)}, bf16[1024,256]{1,0:T(8,128)(2,1)S(1)}, u32[]{:S(2)}, u32[]{:S(2)}) collective-permute-start(bf16[1024,256]{1,0:T(8,128)(2,1)S(1)} %get-tuple-element.15), channel_id=1, source_target_pairs={{0,4},{4,0},{8,12},{12,8},{16,20},{20,16},{24,28},{28,24},{1,5},{5... | collective-permute-start | bytes 1572872 | tf_op jit(solution)/shard_map/ppermute | solution.py:258
  58.0 14.3 %collective-permute-start.19 = (bf16[320,256]{1,0:T(8,128)(2,1)S(1)}, bf16[320,256]{1,0:T(8,128)(2,1)S(1)}, u32[]{:S(2)}, u32[]{:S(2)}) collective-permute-start(bf16[320,256]{1,0:T(8,128)(2,1)S(1)} %get-tuple-element.18.refs_0_), channel_id=1, source_target_pairs={{0,16},{4,20},{8,24},{12,28},{16,0},{20,4},{24,8},{28,12},{1,17},{... | collective-permute-start | bytes 491528 | tf_op jit(solution)/shard_map/ppermute | solution.py:314
  58.0 21.8 %collective-permute-start.14 = (bf16[1024,256]{1,0:T(8,128)(2,1)S(1)}, bf16[1024,256]{1,0:T(8,128)(2,1)S(1)}, u32[]{:S(2)}, u32[]{:S(2)}) collective-permute-start(bf16[1024,256]{1,0:T(8,128)(2,1)S(1)} %collective-permute-done.13.refs_7_), channel_id=1, source_target_pairs={{0,8},{8,16},{16,24},{12,4},{20,12},{28,20},{1,9},{9,17},{17,25},{... | collective-permute-start | bytes 1572872 | tf_op jit(solution)/shard_map/ppermute | solution.py:263
  61.3 29.8 %collective-permute-start.15 = (bf16[1024,256]{1,0:T(8,128)(2,1)S(1)}, bf16[1024,256]{1,0:T(8,128)(2,1)S(1)}, u32[]{:S(2)}, u32[]{:S(2)}) collective-permute-start(bf16[1024,256]{1,0:T(8,128)(2,1)S(1)} %collective-permute-done.12.refs_6_), channel_id=1, source_target_pairs={{0,8},{8,16},{16,24},{12,4},{20,12},{28,20},{1,9},{9,17},{17,25},{... | collective-permute-start | bytes 1572872 | tf_op jit(solution)/shard_map/ppermute | solution.py:263
  63.2 9.1 %copy-start.2 = (bf16[256,1024]{1,0:T(8,128)(2,1)S(1)}, bf16[256,1024]{1,0:T(8,128)(2,1)}, u32[]{:S(2)}) copy-start(bf16[256,1024]{1,0:T(8,128)(2,1)} %refs_8_.1) | copy-start | bytes 1572868
  73.5 28.9 %collective-permute-start.11 = (bf16[1024,256]{1,0:T(8,128)(2,1)S(1)}, bf16[1024,256]{1,0:T(8,128)(2,1)S(1)}, u32[]{:S(2)}, u32[]{:S(2)}) collective-permute-start(bf16[1024,256]{1,0:T(8,128)(2,1)S(1)} %collective-permute-done.10.refs_8_), channel_id=1, source_target_pairs={{0,8},{8,16},{16,24},{12,4},{20,12},{28,20},{1,9},{9,17},{17,25},{... | collective-permute-start | bytes 1572872 | tf_op jit(solution)/shard_map/ppermute | solution.py:263
  75.4 38.2 %collective-permute-start.9 = (bf16[1024,256]{1,0:T(8,128)(2,1)S(1)}, bf16[1024,256]{1,0:T(8,128)(2,1)S(1)}, u32[]{:S(2)}, u32[]{:S(2)}) collective-permute-start(bf16[1024,256]{1,0:T(8,128)(2,1)S(1)} %collective-permute-done.8.refs_7_), channel_id=1, source_target_pairs={{0,8},{8,16},{16,24},{12,4},{20,12},{28,20},{1,9},{9,17},{17,25},{... | collective-permute-start | bytes 1572872 | tf_op jit(solution)/shard_map/ppermute | solution.py:263
